TPU v7x, 128 devices: a whole 4x4x4 slice. The times are simulated.
128 devices in a mesh: front: 4 (over y), sub: 32 (over x, z, core).
Axes of the slice: x: 4, y: 4, z: 4, core: 2. Of those that a mesh axis runs over, the one named last changes fastest.
Arguments:
- front: float32 [16, 4096, 2048], P('front', 'sub'), parts along dimension 0, may hold values from -8 to 1208
- children: float32 [24, 4096, 2048], P('front', 'sub'), parts along dimension 0, may hold values from -0.5 to 0.5
- row_maps: int32 [8, 96], P('front'), parts along dimension 0, may hold values from 0 to 127, as said below
Outputs:
- panel: float32 [16, 4096, 256], P('front', 'sub'), parts along dimension 0
- update: float32 [16, 4096, 1792], P('front', 'sub'), parts along dimension 0
There are 4 independent parts, one for each index of `front`. A program takes and returns all parts, laid end to end along the dimension named above; each array names one. Nothing has to cross between parts.
Inputs may be any that keep to these rules, and one draw needn't show every extreme that they name: row_maps[k, b] and b agree modulo 16; the entries of one child are distinct; for each residue i below 16 each child has exactly one block mapped to i and one mapped to i + 16; among each child's blocks of one residue exactly 3 are mapped to blocks p with p // 16 even.
All inputs are finite; a program needn't handle non-finite values.
Results may differ from a plain program's by a relative error of at most 0.00009.
Values sent between devices are 32-bit elements; how exact they have to be, the bound alone decides.
No kernel may reach another device: no remote copies, remote signals or barrier semaphores. Data moves between devices by JAX's collectives and lax.ppermute only.
A program may use at most 128 MiB of HBM per device.

v0:
```python
import jax
import jax.numpy as jnp
from jax import lax
from jax.sharding import PartitionSpec as P

PANEL = 256


far_away = 1 << 20


def from_partner(block, axis, bit):
    count = lax.axis_size(axis)
    route = []
    for low in range(count):
        high = low | 1 << bit
        if high != low and high < count:
            route += [(low, high), (high, low)]
    return lax.ppermute(block, axis, route)


def place_blocks(blocks, slots, slot_count):
    one_hot = (jnp.arange(slot_count, dtype=jnp.int32)[:, None] == slots[None, :]).astype(
        jnp.float32
    )
    return jnp.einsum("ps,sbw->pbw", one_hot, blocks, precision=lax.Precision.HIGHEST)


def per_device(front, children, row_maps):
    sub_size = lax.axis_size("sub")
    half_size = sub_size // 2
    top_bit = sub_size.bit_length() - 2
    device = lax.axis_index("sub")
    sibling = device // half_size
    residue = device % half_size
    slot_count = front.shape[0]
    block_rows = front.shape[1]
    columns = front.shape[2]
    child_slots = children.shape[0]
    moving = child_slots // 2
    my_targets = jnp.take(row_maps[sibling].reshape(child_slots, half_size), residue, axis=1)
    their_targets = jnp.take(row_maps[1 - sibling].reshape(child_slots, half_size), residue, axis=1)
    my_steps = (my_targets - residue) // half_size
    their_steps = (their_targets - residue) // half_size
    out_index = jnp.argsort(jnp.where(my_steps % 2 != sibling, my_steps, far_away), stable=True)[
        :moving
    ]
    keep_index = jnp.argsort(jnp.where(my_steps % 2 == sibling, my_steps, far_away), stable=True)[
        :moving
    ]
    in_index = jnp.argsort(
        jnp.where(their_steps % 2 == sibling, their_steps, far_away), stable=True
    )[:moving]
    keep_slots = my_steps[keep_index] // 2
    incoming_slots = their_steps[in_index] // 2
    outgoing = children[out_index]
    kept_blocks = children[keep_index]
    all_slots = jnp.concatenate([keep_slots, incoming_slots])
    incoming = from_partner(outgoing, "sub", top_bit)
    assembled = front + place_blocks(
        jnp.concatenate([kept_blocks, incoming]), all_slots, slot_count
    )
    pieces = assembled[0][:, :PANEL]
    gathered = lax.all_gather(pieces, "sub", axis=0, tiled=True)
    window = gathered[:columns]
    diag_block = window[:PANEL]
    lower_factor = jnp.linalg.cholesky(0.5 * (diag_block + diag_block.T))
    window_panel = jax.scipy.linalg.solve_triangular(lower_factor, window[PANEL:].T, lower=True).T
    lower_factor, window_panel = (lower_factor, window_panel)
    local_rows = assembled.reshape(slot_count * block_rows, columns)
    local_panel = jax.scipy.linalg.solve_triangular(
        lower_factor, local_rows[:, :PANEL].T, lower=True
    ).T
    update = local_rows[:, PANEL:] - jnp.dot(
        local_panel, window_panel.T, precision=lax.Precision.HIGHEST
    )
    return (
        local_panel.reshape(slot_count, block_rows, PANEL),
        update.reshape(slot_count, block_rows, columns - PANEL),
    )


def solution(mesh):
    placed = (P("front", "sub", None), P("front", "sub", None), P("front", None))
    return jax.shard_map(
        per_device,
        mesh=mesh,
        in_specs=placed,
        out_specs=(P("front", "sub", None), P("front", "sub", None)),
        check_vma=False,
    )
```

profile of v0, /device:TPU:0, one launch (start us, length us, event | category | flops | bytes accessed | tf_op | source)
XLA Modules:
  0.0 243.9 jit_solution(2019815639375200644)
XLA Ops:
  7.2 0.0 all-gather.2.cloned.1.call-start
  7.3 0.8 fusion.25
  8.0 0.1 reshape_squeeze.6
  8.1 0.2 select_reduce_fusion.3
  8.3 0.1 reshape_squeeze.7
  8.4 0.2 select_reduce_fusion.2
  8.6 1.0 sort.47
  9.6 1.0 sort.46
  10.6 5.2 %gather_fusion.3 = f32[3,128,2048]{2,1,0:T(8,128)} fusion(f32[6,128,2048]{2,1,0:T(8,128)} %param.6, s32[1024]{0:T(1024)S(1)} %pad_clamp_fusion), kind=kCustom, calls=%fused_computation.3 | custom fusion | bytes 6291468 | tf_op jit(solution)/shard_map/gather | solution.py:56
  15.8 3.1 %collective-permute-start = (f32[3,128,2048]{2,1,0:T(8,128)}, f32[3,128,2048]{2,1,0:T(8,128)}, u32[]{:S(2)}, u32[]{:S(2)}) collective-permute-start(f32[3,128,2048]{2,1,0:T(8,128)} %gather_fusion.3), channel_id=1, source_target_pairs={{0,16},{16,0},{1,17},{17,1},{2,18},{18,2},{3,19},{19,3},{4,20},{20... | collective-permute-start | bytes 9437192 | tf_op jit(solution)/shard_map/ppermute | solution.py:19
  18.9 1.0 sort.45
  19.9 3.5 %gather_fusion.2 = f32[3,128,2048]{2,1,0:T(8,128)S(1)} fusion(f32[6,128,2048]{2,1,0:T(8,128)} %param.6, s32[1024]{0:T(1024)S(1)} %pad_clamp_fusion.2), kind=kCustom, calls=%fused_computation.2 | custom fusion | bytes 6291468 | tf_op jit(solution)/shard_map/gather | solution.py:57
  23.4 0.6 gather_fusion
  24.0 4.1 %copy.18 = f32[3,128,2048]{2,0,1:T(4,128)} copy(f32[3,128,2048]{2,1,0:T(8,128)S(1)} %gather_fusion.2) | data formatting | bytes 6291456 | tf_op jit(solution)/shard_map/gather | solution.py:57
  28.2 5.3 %copy.20 = f32[4,128,2048]{1,2,0:T(8,128)} copy(f32[4,128,2048]{2,1,0:T(8,128)} %param.5) | data formatting | bytes 8388608 | tf_op args[0]
  33.5 0.6 gather_fusion.1
  34.2 0.0 copy-start.1
  34.2 0.1 pad_add_fusion
  34.3 53.0 %collective-permute-done = f32[3,128,2048]{2,1,0:T(8,128)} collective-permute-done((f32[3,128,2048]{2,1,0:T(8,128)}, f32[3,128,2048]{2,1,0:T(8,128)}, u32[]{:S(2)}, u32[]{:S(2)}) %collective-permute-start) | collective-permute-done | bytes 3145760 | tf_op jit(solution)/shard_map/ppermute | solution.py:19
  87.3 4.0 %copy.19 = f32[3,128,2048]{2,0,1:T(4,128)S(1)} copy(f32[3,128,2048]{2,1,0:T(8,128)} %collective-permute-done) | data formatting | bytes 6291456 | tf_op jit(solution)/shard_map/ppermute | solution.py:19
  91.3 0.0 copy-done.1
  91.4 7.0 %fusion = f32[4,128,2048]{2,0,1:T(4,128)} fusion(f32[3,128,2048]{2,0,1:T(4,128)S(1)} %copy.19, f32[3,128,2048]{2,0,1:T(4,128)S(1)} %copy-done.1, s32[6]{0:T(128)S(1)} %pad_add_fusion), kind=kOutput, calls=%fused_computation.6 | convolution fusion | flops 77070360 | bytes 10485784 | tf_op jit(solution)/shard_map/ps,sbw->pbw/dot_general | solution.py:26
  98.3 5.3 %copy.21 = f32[4,128,2048]{1,2,0:T(8,128)} copy(f32[4,128,2048]{2,0,1:T(4,128)} %fusion) | data formatting | bytes 8388608 | tf_op jit(solution)/shard_map/ps,sbw->pbw/dot_general | solution.py:26
  103.6 3.9 %add.81 = f32[4,128,2048]{1,2,0:T(8,128)S(1)} add(f32[4,128,2048]{1,2,0:T(8,128)} %copy.20, f32[4,128,2048]{1,2,0:T(8,128)} %copy.21) | non-fusion elementwise | flops 1048576 | bytes 12582912 | tf_op jit(solution)/shard_map/add | solution.py:60
  107.5 0.0 copy-start
  107.5 2.0 copy-done
  109.5 0.1 slice_bitcast_fusion.1
  109.5 0.7 slice.128
  110.2 0.0 all-gather.2.cloned.1.call-update
  110.3 5.4 %copy.24 = f32[4,128,2048]{2,1,0:T(8,128)} copy(f32[4,128,2048]{1,2,0:T(8,128)} %copy-done) | data formatting | bytes 8388608 | tf_op jit(solution)/shard_map/add | solution.py:60
  115.7 1.1 slice.130
  116.8 0.2 copy.28
  117.0 45.4 %all-gather.2.cloned.1.call-done = f32[4096,256]{0,1:T(8,128)} async-done(((f32[128,256]{0,1:T(8,128)}), f32[4096,256]{0,1:T(8,128)}) %all-gather.2.cloned.1.call-update) | async-done | bytes 4194320 | tf_op jit(solution)/shard_map/all_gather | solution.py:64
  162.4 1.0 slice.129
  163.3 0.1 copy.22
  163.5 1.0 fusion.13
  164.5 0.1 copy.23
  164.7 11.7 %cholesky.50 = f32[128,128]{1,0:T(8,128)S(1)} custom-call(f32[128,128]{1,0:T(8,128)S(1)} %cholesky.118), custom_call_target="Cholesky" | custom-call | tf_op jit(solution)/shard_map/jit(cholesky)/cholesky | solution.py:67
  176.4 9.8 %custom-call.18 = f32[1,128,128]{1,2,0:T(8,128)S(1)} custom-call(f32[1,128,128]{2,1,0:T(8,128)S(1)} %get-tuple-element.54), custom_call_target="InvertDiagBlocksLowerTriangular" | custom-call | tf_op jit(solution)/shard_map/jit(cholesky)/cholesky | solution.py:67
  186.3 0.2 constant_dynamic-update-slice_fusion
  186.5 0.3 convolution_subtract_fusion.2
  186.7 11.7 %cholesky.105 = f32[128,128]{1,0:T(8,128)S(1)} custom-call(f32[128,128]{1,0:T(8,128)S(1)} %convolution_subtract_fusion.2), custom_call_target="Cholesky" | custom-call | tf_op jit(solution)/shard_map/jit(cholesky)/cholesky | solution.py:67
  198.5 0.6 compare_reduce_fusion
  199.1 0.6 compare_reduce_fusion.1
  201.1 0.1 triangular_solve.72
  201.2 4.0 %while.2 = (s32[]{:T(128)}, f32[256,256]{1,0:T(8,128)S(1)}, s32[2,2]{1,0:T(2,128)S(1)}, f32[2,128,128]{2,1,0:T(8,128)S(1)}, s32[]{:T(128)}) while((s32[]{:T(128)}, f32[256,256]{1,0:T(8,128)S(1)}, s32[2,2]{1,0:T(2,128)S(1)}, f32[2,128,128]{2,1,0:T(8,128)S(1)}, s32[]{:T(128)}) %tuple.40), condition=%wide.while_cond.1, body=%wide.while_body.1.sunk | while | flops 2 | bytes 131181 | solution.py:71
  201.2 0.6 fusion.38
  201.8 1.4 bitcast_dynamic-update-slice_fusion.2
  203.2 0.6 fusion.38
  203.8 1.4 bitcast_dynamic-update-slice_fusion.2
  205.2 19.9 %custom-call.19 = f32[2,128,128]{1,2,0:T(8,128)S(1)} custom-call(f32[2,128,128]{2,1,0:T(8,128)S(1)} %get-tuple-element.24), custom_call_target="InvertDiagBlocksLowerTriangular" | custom-call | tf_op jit(solution)/shard_map/jit(_solve_triangular)/triangular_solve | solution.py:71
  225.1 1.6 slice_bitcast_fusion
  226.7 1.0 fusion.7
  227.7 0.0 copy-start.2
  227.7 0.9 convolution_subtract_fusion
  228.6 0.9 fusion.17
  229.5 0.4 fusion.10
  229.9 0.4 convolution_subtract_fusion.1
  230.3 0.4 fusion.18
  230.8 0.0 copy-done.2
  230.8 5.3 %slice_subtract_fusion = f32[512,1792]{1,0:T(8,128)} fusion(f32[512,2048]{1,0:T(8,128)S(1)} %bitcast.53, f32[128,1792]{1,0:T(8,128)S(1)} %fusion.17, f32[128,1792]{1,0:T(8,128)S(1)} %fusion.7, f32[128,512]{1,0:T(8,128)S(1)} %fusion.18, f32[128,512]{1,0:T(8,128)S(1)} %fusion.10), kind=kOutput, calls=%fused_computation.10 | convolution fusion | flops 2820079616 | bytes 9699328 | tf_op jit(solution)/shard_map/dot_general | solution.py:74
  236.1 1.0 copy.27
  (24 shorter events, 0.3 us)
Async XLA Ops:
  7.2 155.2 %all-gather.2.cloned.1.call-start = ((), (), s32[]{:S(2)}) async-start(), calls=%async_computation | async-start | bytes 4325376 | tf_op jit(solution)/shard_map/all_gather | solution.py:64
  15.8 71.5 %collective-permute-start = (f32[3,128,2048]{2,1,0:T(8,128)}, f32[3,128,2048]{2,1,0:T(8,128)}, u32[]{:S(2)}, u32[]{:S(2)}) collective-permute-start(f32[3,128,2048]{2,1,0:T(8,128)} %gather_fusion.3), channel_id=1, source_target_pairs={{0,16},{16,0},{1,17},{17,1},{2,18},{18,2},{3,19},{19,3},{4,20},{20... | collective-permute-start | bytes 9437192 | tf_op jit(solution)/shard_map/ppermute | solution.py:19
  34.2 57.2 %copy-start.1 = (f32[3,128,2048]{2,0,1:T(4,128)S(1)}, f32[3,128,2048]{2,0,1:T(4,128)}, u32[]{:S(2)}) copy-start(f32[3,128,2048]{2,0,1:T(4,128)} %copy.18) | copy-start | bytes 9437188
  107.5 2.0 copy-start
  227.7 3.1 %copy-start.2 = (f32[4,128,2048]{2,1,0:T(8,128)S(1)}, f32[4,128,2048]{2,1,0:T(8,128)}, u32[]{:S(2)}) copy-start(f32[4,128,2048]{2,1,0:T(8,128)} %copy.24) | copy-start | bytes 12582916
Sparse Core Ops, SparseCore 0:
  110.4 51.9 all-gather.1
where the time goes:
time: 246 us; the launch traced here: 244 us
  waiting for transfers between devices  98.5 us (40%)
  other arithmetic  62.9 us (26%)
  local copies, waits for them, and re-layouts  47.1 us (19%)
  matrix products  16.7 us (7%)
  between operations  15.6 us (6%)
  starting transfers between devices  3.14 us (1%)
    ppermute x1, waiting for transfers between devices, from_partner(): return lax.ppermute(block, axis, route)  53 us
    all_gather x1, waiting for transfers between devices, per_device(): gathered = lax.all_gather(pieces, 'sub', axis=0, tiled=True)  45.4 us
    another operation x7, other arithmetic, per_device(): lower_factor = jnp.linalg.cholesky(0.5 * (diag_block + diag_block.T))  34.6 us
    another operation x3, other arithmetic, per_device(): jax.scipy.linalg.solve_triangular(lower_factor, local_rows[:, :PANEL].T,...  19.9 us
    unnamed x9, local copies, waits for them, and re-layouts  8.52 us
    gather x2, local copies, waits for them, and re-layouts, per_device(): kept_blocks = children[keep_index]  7.66 us
    dot_general x1, matrix products, place_blocks(): jnp.einsum('ps,sbw->pbw', one_hot, blocks, precision=lax.Precision.HIGHEST)  6.95 us
    add x1, local copies, waits for them, and re-layouts, per_device(): front + place_blocks(jnp.concatenate([kept_blocks, incoming]), all_slots,...  5.42 us
  transfers between devices with their start and end apart: 2, of which 2 were waited for; matrix products, arithmetic and copies ran while one was open for 9% of the time, Pallas kernels for 0%

commit v1 on v0

v1 whole, which is shorter than its diff:
```python
import functools

import jax
import jax.numpy as jnp
from jax import lax
from jax.experimental import pallas as pl
from jax.experimental.pallas import tpu as pltpu
from jax.sharding import PartitionSpec as P

PANEL = 256
BLK = 128
HIGHEST = lax.Precision.HIGHEST
VMEM_LIMIT = 60 << 20
GROUP = 64

OUT = 0
SLOT = 4
KEEP = 8
CAME = 12
SMALL = pl.CostEstimate(flops=0, bytes_accessed=0, transcendentals=0)


def matmul(a, b, ca, cb):
    return lax.dot_general(
        a, b, (((ca,), (cb,)), ((), ())), precision=HIGHEST, preferred_element_type=jnp.float32
    )


def any_space():
    return pl.BlockSpec(memory_space=pl.ANY)


def smem_space():
    return pl.BlockSpec(memory_space=pltpu.SMEM)


def params():
    return pltpu.CompilerParams(vmem_limit_bytes=VMEM_LIMIT)


def index_kernel(
    half, slots, maps, front, children, idx, piece, rest, others, base, mine, theirs, old, kept, sem
):
    dev = lax.axis_index("sub")
    sib = dev // half
    res = dev % half
    lead = pl.ds(0, PANEL)
    first = pltpu.make_async_copy(front.at[0, :, lead], old, sem.at[0])
    first.start()
    for step in range(8):
        mine[step] = -1
        theirs[step] = -1
    for b in range(slots):
        mine[(maps[sib, b * half + res] - res) // half] = b
        theirs[(maps[1 - sib, b * half + res] - res) // half] = b
    for i in range(16):
        idx[i] = -1
    n_out = jnp.int32(0)
    n_in = jnp.int32(0)
    none = jnp.int32(0)
    for q in range(4):
        b = mine[2 * q + 1 - sib]
        idx[OUT + n_out] = jnp.maximum(b, 0)
        n_out = n_out + jnp.where(b >= 0, 1, 0)
        idx[KEEP + q] = mine[2 * q + sib]
        t = theirs[2 * q + sib]
        idx[SLOT + n_in] = q
        idx[CAME + q] = jnp.where(t >= 0, n_in, -1)
        n_in = n_in + jnp.where(t >= 0, 1, 0)
        none = jnp.where(t >= 0, none, q)
    idx[SLOT + 3] = none
    keep = idx[KEEP]
    copies = [
        pltpu.make_async_copy(children.at[idx[OUT], :, lead], piece, sem.at[1]),
        pltpu.make_async_copy(children.at[jnp.maximum(keep, 0), :, lead], kept, sem.at[2]),
        pltpu.make_async_copy(
            children.at[idx[OUT], :, pl.ds(PANEL, rest.shape[1])], rest, sem.at[3]
        ),
        pltpu.make_async_copy(children.at[idx[OUT + 1], :, lead], others.at[0], sem.at[4]),
        pltpu.make_async_copy(children.at[idx[OUT + 2], :, lead], others.at[1], sem.at[5]),
    ]
    for copy in copies:
        copy.start()
    first.wait()
    for copy in copies:
        copy.wait()
    base[...] = old[...] + kept[...] * jnp.where(keep >= 0, 1.0, 0.0)


def make_indices(row_maps, front, children, half):
    rest = children.shape[2] - PANEL
    vmem = pl.BlockSpec(memory_space=pltpu.VMEM)
    return pl.pallas_call(
        functools.partial(index_kernel, half, children.shape[0]),
        name="indices",
        out_shape=(
            jax.ShapeDtypeStruct((16,), jnp.int32),
            jax.ShapeDtypeStruct((BLK, PANEL), jnp.float32),
            jax.ShapeDtypeStruct((BLK, rest), jnp.float32),
            jax.ShapeDtypeStruct((2, BLK, PANEL), jnp.float32),
            jax.ShapeDtypeStruct((BLK, PANEL), jnp.float32),
        ),
        in_specs=[smem_space(), any_space(), any_space()],
        out_specs=(smem_space(), vmem, vmem, vmem, vmem),
        scratch_shapes=[
            pltpu.SMEM((8,), jnp.int32),
            pltpu.SMEM((8,), jnp.int32),
            pltpu.VMEM((BLK, PANEL), jnp.float32),
            pltpu.VMEM((BLK, PANEL), jnp.float32),
            pltpu.SemaphoreType.DMA((6,)),
        ],
        compiler_params=params(),
        cost_estimate=SMALL,
    )(row_maps, front, children)


def take_kernel(idx, children, one, two, sem):
    part = pl.ds(PANEL, one.shape[1])
    copies = [
        pltpu.make_async_copy(children.at[idx[OUT + 1 + i], :, part], out, sem.at[i])
        for i, out in enumerate((one, two))
    ]
    for copy in copies:
        copy.start()
    for copy in copies:
        copy.wait()


def take_blocks(idx, children):
    shape = jax.ShapeDtypeStruct((BLK, children.shape[2] - PANEL), jnp.float32)
    vmem = pl.BlockSpec(memory_space=pltpu.VMEM)
    return pl.pallas_call(
        take_kernel,
        name="take",
        out_shape=(shape, shape),
        in_specs=[smem_space(), any_space()],
        out_specs=(vmem, vmem),
        scratch_shapes=[pltpu.SemaphoreType.DMA((2,))],
        compiler_params=params(),
        cost_estimate=SMALL,
    )(idx, children)


def inverse_factor(d):
    n = d.shape[0]
    row = lax.broadcasted_iota(jnp.int32, (n, n), 0)
    col = lax.broadcasted_iota(jnp.int32, (n, n), 1)
    m = jnp.concatenate([d, (row == col).astype(jnp.float32)], axis=1)
    w = 2 * n
    parts = n // 8
    groups = [m[8 * i : 8 * i + 8, :] for i in range(parts)]
    sub = lax.broadcasted_iota(jnp.int32, (8, w), 0)
    for q in range(parts):
        e = [
            [
                jnp.broadcast_to(groups[i][:, 8 * q + k : 8 * q + k + 1], (8, w))
                for i in range(q, parts)
            ]
            for k in range(8)
        ]
        for k in range(8):
            r = lax.rsqrt(jnp.broadcast_to(e[k][0][k : k + 1, :], (8, w)))
            pivot_row = jnp.broadcast_to(groups[q][k : k + 1, :], (8, w)) * r
            scaled = [v * r for v in e[k]]
            for i in range(q, parts):
                t = groups[i] - scaled[i - q] * pivot_row
                if i == q:
                    t = jnp.where(sub == k, pivot_row, jnp.where(sub > k, t, groups[i]))
                groups[i] = t
            for c in range(k + 1, 8):
                head = jnp.broadcast_to(e[c][0][k : k + 1, :], (8, w)) * r
                e[c] = [v - u * head for v, u in zip(e[c], scaled)]
    return jnp.concatenate(groups, axis=0)[:, n:]


def factor_kernel(half, *refs):
    pieces, (inv, wide), (window, m) = refs[:8], refs[8:10], refs[10:]
    dev = lax.axis_index("sub")
    z = (dev // 2) % 4
    core = dev % 2
    for i, ref in enumerate(pieces):
        zz = (z + i // 2) % 4
        cc = (core + i) % 2
        for h in range(2):
            block = (h * 4 + zz) * 2 + cc
            window[pl.ds(pl.multiple_of(block * BLK, BLK), BLK), :] = ref[h]
    s = window[0:PANEL, :]
    s = 0.5 * (s + s.T)
    m[:, :PANEL] = s
    row = lax.broadcasted_iota(jnp.int32, (PANEL, PANEL), 0)
    col = lax.broadcasted_iota(jnp.int32, (PANEL, PANEL), 1)
    m[:, PANEL:] = (row == col).astype(jnp.float32)
    for k in range(PANEL // GROUP):
        a, b = k * GROUP, (k + 1) * GROUP
        r = m[a:b, :]
        x = matmul(inverse_factor(r[:, a:b]), r, 1, 0)
        m[a:b, :] = x
        if b < PANEL:
            m[b:, :] = m[b:, :] - matmul(x[:, b:PANEL], x, 0, 0)
    linv = m[:, PANEL:]
    inv[...] = linv
    wide[...] = matmul(window[PANEL:, :], linv, 1, 1)


def factor(pieces, half, columns):
    return pl.pallas_call(
        functools.partial(factor_kernel, half),
        name="factor",
        out_shape=(
            jax.ShapeDtypeStruct((PANEL, PANEL), jnp.float32),
            jax.ShapeDtypeStruct((columns - PANEL, PANEL), jnp.float32),
        ),
        scratch_shapes=[
            pltpu.VMEM((columns, PANEL), jnp.float32),
            pltpu.VMEM((PANEL, 2 * PANEL), jnp.float32),
        ],
        compiler_params=params(),
        cost_estimate=SMALL,
    )(*pieces)


def base_kernel(slots, idx, *refs):
    fronts, (lead_front,), refs = refs[:1], refs[1:2], refs[2:]
    kept, lead_kept, (came, others, inv, wide, panel, update, held) = (
        refs[:slots], refs[slots : 2 * slots], refs[2 * slots :]
    )
    has = [jnp.where(idx[KEEP + q] >= 0, 1.0, 0.0) for q in range(slots)]

    @pl.when(pl.program_id(0) == 0)
    def _():
        for q in range(slots):
            which = idx[CAME + q]
            second = others[jnp.clip(which - 1, 0, 1)]
            got = jnp.where(which == 0, came[...], jnp.where(which > 0, second, 0.0))
            held[q * BLK : (q + 1) * BLK, :] = (
                lead_front[q] + lead_kept[q][0] * has[q] + got
            )
        p = matmul(held[...], inv[...], 1, 1)
        held[...] = p
        for q in range(slots):
            panel[q] = p[q * BLK : (q + 1) * BLK, :]

    u = matmul(held[...], wide[...], 1, 1)
    for q in range(slots):
        update[q] = fronts[0][q] + kept[q][0] * has[q] - u[q * BLK : (q + 1) * BLK, :]


def make_base(idx, front, children, came, others, inv, wide):
    slots, rows, columns = front.shape
    rest = columns - PANEL
    whole = lambda shape: pl.BlockSpec(shape, lambda i, idx: (0,) * len(shape))
    kept = lambda q, at: pl.BlockSpec(
        (1, rows, PANEL), lambda i, idx: (jnp.maximum(idx[KEEP + q], 0), 0, (i + 1) * at)
    )
    in_specs = (
        [
            pl.BlockSpec((slots, rows, PANEL), lambda i, idx: (0, 0, i + 1)),
            pl.BlockSpec((slots, rows, PANEL), lambda i, idx: (0, 0, 0)),
        ]
        + [kept(q, 1) for q in range(slots)]
        + [kept(q, 0) for q in range(slots)]
        + [
            whole(came.shape),
            whole(others.shape),
            whole(inv.shape),
            pl.BlockSpec((PANEL, PANEL), lambda i, idx: (i, 0)),
        ]
    )
    grid = pltpu.PrefetchScalarGridSpec(
        num_scalar_prefetch=1,
        grid=(rest // PANEL,),
        in_specs=in_specs,
        out_specs=(
            whole((slots, rows, PANEL)),
            pl.BlockSpec((slots, rows, PANEL), lambda i, idx: (0, 0, i)),
        ),
        scratch_shapes=[pltpu.VMEM((slots * rows, PANEL), jnp.float32)],
    )
    return pl.pallas_call(
        functools.partial(base_kernel, slots),
        name="base",
        out_shape=(
            jax.ShapeDtypeStruct((slots, rows, PANEL), jnp.float32),
            jax.ShapeDtypeStruct((slots, rows, rest), jnp.float32),
        ),
        grid_spec=grid,
        compiler_params=params(),
        cost_estimate=SMALL,
    )(idx, *[front] * 2, *[children] * (2 * slots), came, others, inv, wide)


def add_kernel(idx, old, came, out):
    out[0] = old[0] + came[...]


def add_block(idx, update, came, which):
    slots, rows, rest = update.shape
    at_slot = pl.BlockSpec((1, rows, rest), lambda i, idx: (idx[SLOT + which], 0, 0))
    grid = pltpu.PrefetchScalarGridSpec(
        num_scalar_prefetch=1,
        grid=(1,),
        in_specs=[at_slot, pl.BlockSpec(came.shape, lambda i, idx: (0, 0))],
        out_specs=at_slot,
    )
    return pl.pallas_call(
        add_kernel,
        name=f"add{which}",
        out_shape=jax.ShapeDtypeStruct(update.shape, jnp.float32),
        grid_spec=grid,
        input_output_aliases={1: 0},
        compiler_params=params(),
        cost_estimate=SMALL,
    )(idx, update, came)


def route(move, keep=lambda x: True):
    pairs = []
    for x in range(4):
        if keep(x):
            for z in range(4):
                for c in range(2):
                    tx, tz, tc = move(x, z, c)
                    pairs.append(((x * 4 + z) * 2 + c, (tx * 4 + tz) * 2 + tc))
    return pairs


OPPOSITE = route(lambda x, z, c: ((x + 2) % 4, z, c))
SIDE = route(lambda x, z, c: (1 - x, z, c), lambda x: x < 2)
BACK = route(lambda x, z, c: (3 - x, z, c), lambda x: x < 2)
ACROSS = route(lambda x, z, c: (x + 2, z, c), lambda x: x < 2)
Z_UP = route(lambda x, z, c: (x, (z + 1) % 4, c))
Z_DOWN = route(lambda x, z, c: (x, (z + 3) % 4, c))
Z_FAR = route(lambda x, z, c: (x, (z + 2) % 4, c))
CORE = route(lambda x, z, c: (x, z, 1 - c))


def send(value, pairs):
    return lax.ppermute(value, "sub", pairs)


def per_device(front, children, row_maps):
    half = lax.axis_size("sub") // 2
    columns = front.shape[2]
    x = lax.axis_index("sub") // 8

    idx, first, b0, second, base_lead = make_indices(row_maps, front, children, half)
    came_first = send(first, OPPOSITE)
    came_others = send(second, OPPOSITE)
    b1, b2 = take_blocks(idx, children)
    came = [send(b, OPPOSITE) for b in (b0, b1, b2)]

    lead = base_lead + came_first
    side, back, across = send(lead, SIDE), send(lead, BACK), send(lead, ACROSS)
    row_a = jnp.where(x == 0, lead, jnp.where(x == 1, side, jnp.where(x == 2, across, back)))
    row_b = jnp.where(x == 1, lead, jnp.where(x == 0, side, jnp.where(x == 3, across, back)))
    own = jnp.stack([row_a, row_b])

    by_z = [own, send(own, Z_DOWN), send(own, Z_FAR), send(own, Z_UP)]
    pieces = []
    for v in by_z:
        pieces += [v, send(v, CORE)]
    inv, wide = factor(pieces, half, columns)

    panel, update = make_base(idx, front, children, came_first, came_others, inv, wide)
    for which, block in enumerate(came):
        update = add_block(idx, update, block, which)
    return panel, update


def solution(mesh):
    placed = (P("front", "sub", None), P("front", "sub", None), P("front", None))
    return jax.shard_map(
        per_device,
        mesh=mesh,
        in_specs=placed,
        out_specs=(P("front", "sub", None), P("front", "sub", None)),
        check_vma=False,
    )
```

time: 246 us -> 122 us (0.50)
  other arithmetic: 62.9 us -> 1.02 us
  waiting for transfers between devices: 98.5 us -> 49.5 us
  local copies, waits for them, and re-layouts: 47.1 us -> 4.23 us
  Pallas kernels: 0 us -> 41.5 us
  starting transfers between devices: 3.14 us -> 23.8 us
  matrix products: 16.7 us -> 0 us
  between operations: 15.6 us -> 0.82 us
    another operation x10 -> x2, other arithmetic: 54.5 us -> 0.05 us  [per_device(): own = jnp.stack([row_a, row_b])]
    all_gather x1 -> x0, waiting for transfers between devices: 45.4 us -> none  [per_device(): gathered = lax.all_gather(pieces, 'sub', axis=0, tiled=True)]
    pallas_call x0 -> x7, Pallas kernels: none -> 41.5 us  [the longest x1 14.1 us: factor(): pl.pallas_call(functools.partial(factor_kernel, half), name='factor', out...]
    ppermute x1 -> x15, starting transfers between devices: 3.11 us -> 23.8 us  [send(): return lax.ppermute(value, 'sub', pairs)]
    gather x5 -> x0, local copies, waits for them, and re-layouts: 14.1 us -> none  [the longest x2 7.66 us: per_device(): kept_blocks = children[keep_index]]
    dot_general x2 -> x0, matrix products: 12.2 us -> none  [the longest x1 6.95 us: place_blocks(): jnp.einsum('ps,sbw->pbw', one_hot, blocks, precision=lax.Precision.HIGHEST)]
    add x1 -> x0, local copies, waits for them, and re-layouts: 5.42 us -> none  [per_device(): front + place_blocks(jnp.concatenate([kept_blocks, incoming]), all_slots,...]
    dot_general x1 -> x0, local copies, waits for them, and re-layouts: 5.31 us -> none  [place_blocks(): jnp.einsum('ps,sbw->pbw', one_hot, blocks, precision=lax.Precision.HIGHEST)]
  transfers between devices with their start and end apart: 2 -> 15, of which waited for: 2 -> 8; matrix products, arithmetic and copies ran while one was open for 9% -> 0% of each run, Pallas kernels for 0% -> 29%
where the time goes in v1:
time: 122 us; the launch traced here: 121 us
  waiting for transfers between devices  49.5 us (41%)
  Pallas kernels  41.5 us (34%)
  starting transfers between devices  23.8 us (20%)
  local copies, waits for them, and re-layouts  4.23 us (3%)
    ppermute x15, waiting for transfers between devices, send(): return lax.ppermute(value, 'sub', pairs)  49.5 us
    ppermute x15, starting transfers between devices, send(): return lax.ppermute(value, 'sub', pairs)  23.8 us
    pallas_call x1, Pallas kernels, factor(): pl.pallas_call(functools.partial(factor_kernel, half), name='factor', out...  14.1 us
    pallas_call x1, Pallas kernels, make_base(): pl.pallas_call(functools.partial(base_kernel, slots), name='base', out_sh...  11.2 us
    pallas_call x3, Pallas kernels, add_block(): pl.pallas_call(add_kernel, name=f'add{which}', out_shape=jax.ShapeDtypeSt...  9.4 us
    unnamed x24, local copies, waits for them, and re-layouts  4.23 us
    pallas_call x1, Pallas kernels, take_blocks(): pl.pallas_call(take_kernel, name='take', out_shape=(shape, shape), in_spe...  3.38 us
    pallas_call x1, Pallas kernels, make_indices(): pl.pallas_call(functools.partial(index_kernel, half, children.shape[0]),...  3.32 us
  transfers between devices with their start and end apart: 15, of which 8 were waited for; matrix products, arithmetic and copies ran while one was open for 0% of the time, Pallas kernels for 29%

profile of v1, /device:TPU:0, one launch (start us, length us, event | category | flops | bytes accessed | tf_op | source)
XLA Modules:
  0.0 120.8 jit_solution(10390594941831140579)
XLA Ops:
  0.6 3.3 %indices.1 = (s32[16]{0:T(128)}, f32[128,256]{1,0:T(8,128)}, f32[128,1792]{1,0:T(8,128)}, f32[2,128,256]{2,1,0:T(8,128)}, f32[128,256]{1,0:T(8,128)}) custom-call(s32[2,96]{1,0:T(2,128)} %maps.1, f32[4,128,2048]{2,1,0:T(8,128)} %refs_1_.1, f32[6,128,2048]{2,1,0:T(8,128)} %children.3), custom_call_target="tpu_custom_call" | custom-call | tf_op jit(solution)/shard_map/indices/pallas_call | solution.py:93
  4.0 3.2 %collective-permute-start = (f32[128,256]{1,0:T(8,128)}, f32[128,256]{1,0:T(8,128)S(1)}, u32[]{:S(2)}, u32[]{:S(2)}) collective-permute-start(f32[128,256]{1,0:T(8,128)} %get-tuple-element.14), channel_id=1, source_target_pairs={{0,16},{1,17},{2,18},{3,19},{4,20},{5,21},{6,22},{7,23},{8,24},{9,... | collective-permute-start | bytes 393224 | tf_op jit(solution)/shard_map/ppermute | solution.py:338
  7.1 3.7 %collective-permute-done.refs_10_ = f32[128,256]{1,0:T(8,128)S(1)} collective-permute-done((f32[128,256]{1,0:T(8,128)}, f32[128,256]{1,0:T(8,128)S(1)}, u32[]{:S(2)}, u32[]{:S(2)}) %collective-permute-start) | collective-permute-done | bytes 131104 | tf_op jit(solution)/shard_map/ppermute | solution.py:338
  10.9 0.0 copy-start.4
  10.9 1.0 add.4
  11.8 3.6 %collective-permute-start.2 = (f32[128,256]{1,0:T(8,128)S(1)}, f32[128,256]{1,0:T(8,128)S(1)}, u32[]{:S(2)}, u32[]{:S(2)}) collective-permute-start(f32[128,256]{1,0:T(8,128)S(1)} %add.4), channel_id=1, source_target_pairs={{0,8},{1,9},{2,10},{3,11},{4,12},{5,13},{6,14},{7,15},{8,0},{9,1},... | collective-permute-start | bytes 393224 | tf_op jit(solution)/shard_map/ppermute | solution.py:338
  15.5 2.2 %collective-permute-start.3 = (f32[128,256]{1,0:T(8,128)S(1)}, f32[128,256]{1,0:T(8,128)S(1)}, u32[]{:S(2)}, u32[]{:S(2)}) collective-permute-start(f32[128,256]{1,0:T(8,128)S(1)} %add.4), channel_id=1, source_target_pairs={{0,16},{1,17},{2,18},{3,19},{4,20},{5,21},{6,22},{7,23},{8,24},{9,... | collective-permute-start | bytes 393224 | tf_op jit(solution)/shard_map/ppermute | solution.py:338
  17.7 1.3 %collective-permute-start.4 = (f32[128,256]{1,0:T(8,128)S(1)}, f32[128,256]{1,0:T(8,128)S(1)}, u32[]{:S(2)}, u32[]{:S(2)}) collective-permute-start(f32[128,256]{1,0:T(8,128)S(1)} %add.4), channel_id=1, source_target_pairs={{0,24},{1,25},{2,26},{3,27},{4,28},{5,29},{6,30},{7,31},{8,16},{9,... | collective-permute-start | bytes 393224 | tf_op jit(solution)/shard_map/ppermute | solution.py:338
  19.0 0.7 collective-permute-done.2
  19.7 1.1 collective-permute-done.3
  20.8 2.2 %collective-permute-done.4 = f32[128,256]{1,0:T(8,128)S(1)} collective-permute-done((f32[128,256]{1,0:T(8,128)S(1)}, f32[128,256]{1,0:T(8,128)S(1)}, u32[]{:S(2)}, u32[]{:S(2)}) %collective-permute-start.4) | collective-permute-done | bytes 131104 | tf_op jit(solution)/shard_map/ppermute | solution.py:338
  23.0 0.0 copy-start
  23.0 0.1 collective-permute-start.5
  23.1 4.1 %collective-permute-start.6 = (f32[2,128,256]{2,1,0:T(8,128)S(1)}, f32[2,128,256]{2,1,0:T(8,128)S(1)}, u32[]{:S(2)}, u32[]{:S(2)}) collective-permute-start(f32[2,128,256]{2,1,0:T(8,128)S(1)} %pad_maximum_fusion.refs_0_), channel_id=1, source_target_pairs={{0,6},{1,7},{2,0},{3,1},{4,2},{5,3},{6,4},{7,5},{8,14},{9,15},{10,... | collective-permute-start | bytes 786440 | tf_op jit(solution)/shard_map/ppermute | solution.py:338
  27.3 3.5 %collective-permute-start.12 = (f32[128,1792]{1,0:T(8,128)}, f32[128,1792]{1,0:T(8,128)S(1)}, u32[]{:S(2)}, u32[]{:S(2)}) collective-permute-start(f32[128,1792]{1,0:T(8,128)} %get-tuple-element.21), channel_id=1, source_target_pairs={{0,16},{1,17},{2,18},{3,19},{4,20},{5,21},{6,22},{7,23},{8,24},{9,... | collective-permute-start | bytes 2752520 | tf_op jit(solution)/shard_map/ppermute | solution.py:338
  30.8 3.4 %take.1 = (f32[128,1792]{1,0:T(8,128)}, f32[128,1792]{1,0:T(8,128)}) custom-call(s32[16]{0:T(128)} %get-tuple-element.13.idx, f32[6,128,2048]{2,1,0:T(8,128)} %children.3), custom_call_target="tpu_custom_call" | custom-call | tf_op jit(solution)/shard_map/take/pallas_call | solution.py:132
  34.2 0.0 copy-done.4
  34.2 0.1 collective-permute-start.13
  34.3 3.5 %collective-permute-start.14 = (f32[128,1792]{1,0:T(8,128)}, f32[128,1792]{1,0:T(8,128)S(1)}, u32[]{:S(2)}, u32[]{:S(2)}) collective-permute-start(f32[128,1792]{1,0:T(8,128)} %get-tuple-element.23), channel_id=1, source_target_pairs={{0,16},{1,17},{2,18},{3,19},{4,20},{5,21},{6,22},{7,23},{8,24},{9,... | collective-permute-start | bytes 2752520 | tf_op jit(solution)/shard_map/ppermute | solution.py:338
  37.8 0.0 collective-permute-done.5.refs_1_
  37.8 0.0 copy-start.6
  37.8 0.0 collective-permute-start.8
  37.8 0.0 collective-permute-done.6.refs_2_
  37.8 0.0 copy-start.7
  37.8 1.2 %collective-permute-start.10 = (f32[2,128,256]{2,1,0:T(8,128)S(1)}, f32[2,128,256]{2,1,0:T(8,128)S(1)}, u32[]{:S(2)}, u32[]{:S(2)}) collective-permute-start(f32[2,128,256]{2,1,0:T(8,128)S(1)} %pad_maximum_fusion.refs_0_), channel_id=1, source_target_pairs={{0,2},{1,3},{2,4},{3,5},{4,6},{5,7},{6,0},{7,1},{8,10},{9,11},{10,... | collective-permute-start | bytes 786440 | tf_op jit(solution)/shard_map/ppermute | solution.py:338
  39.1 9.5 %collective-permute-done.8.refs_4_ = f32[2,128,256]{2,1,0:T(8,128)S(1)} collective-permute-done((f32[2,128,256]{2,1,0:T(8,128)S(1)}, f32[2,128,256]{2,1,0:T(8,128)S(1)}, u32[]{:S(2)}, u32[]{:S(2)}) %collective-permute-start.8) | collective-permute-done | bytes 262176 | tf_op jit(solution)/shard_map/ppermute | solution.py:338
  48.6 0.0 copy-start.8
  48.6 0.0 collective-permute-start.7
  48.6 3.7 %collective-permute-done.10.refs_6_ = f32[2,128,256]{2,1,0:T(8,128)S(1)} collective-permute-done((f32[2,128,256]{2,1,0:T(8,128)S(1)}, f32[2,128,256]{2,1,0:T(8,128)S(1)}, u32[]{:S(2)}, u32[]{:S(2)}) %collective-permute-start.10) | collective-permute-done | bytes 262176 | tf_op jit(solution)/shard_map/ppermute | solution.py:338
  52.3 0.0 copy-start.9
  52.3 0.0 collective-permute-start.9
  52.3 0.0 collective-permute-done.7.refs_3_
  52.3 0.0 copy-start.10
  52.3 0.5 collective-permute-start.11
  52.8 1.0 collective-permute-done.9.refs_5_
  53.8 0.0 copy-done.9
  53.8 0.0 copy-done.10
  53.8 0.0 copy-start.11
  53.8 0.7 copy-done.11
  54.5 0.4 collective-permute-start.1
  54.9 0.0 collective-permute-done.11.refs_7_
  54.9 0.0 copy-done
  54.9 0.0 copy-done.6
  54.9 0.0 copy-done.7
  54.9 0.0 copy-done.8
  54.9 14.1 %factor.1 = (f32[256,256]{1,0:T(8,128)}, f32[1792,256]{1,0:T(8,128)}) custom-call(f32[2,128,256]{2,1,0:T(8,128)} %copy-done, f32[2,128,256]{2,1,0:T(8,128)} %copy-done.6, f32[2,128,256]{2,1,0:T(8,128)} %copy-done.7, f32[2,128,256]{2,1,0:T(8,128)} %copy-done.10, f32[2,128,256]{2,1,0:T(8,128)} %copy-done.8, f32[2,128,256]{2,1,0:T(8,128)} %copy-done.11, ...), custom_call_target="tpu_custom_call" | custom-call | tf_op jit(solution)/shard_map/factor/pallas_call | solution.py:206
  69.1 27.6 %collective-permute-done.1.refs_11_ = f32[2,128,256]{2,1,0:T(8,128)S(1)} collective-permute-done((f32[2,128,256]{2,1,0:T(8,128)}, f32[2,128,256]{2,1,0:T(8,128)S(1)}, u32[]{:S(2)}, u32[]{:S(2)}) %collective-permute-start.1) | collective-permute-done | bytes 262176 | tf_op jit(solution)/shard_map/ppermute | solution.py:338
  96.6 0.0 copy-start.5
  96.6 0.7 copy-done.5
  97.3 11.2 %base.1 = (f32[4,128,256]{2,1,0:T(8,128)}, f32[4,128,1792]{2,1,0:T(8,128)}) custom-call(s32[16]{0:T(128)} %get-tuple-element.13.idx, f32[4,128,2048]{2,1,0:T(8,128)} %refs_1_.1, f32[4,128,2048]{2,1,0:T(8,128)} %refs_1_.1, f32[6,128,2048]{2,1,0:T(8,128)} %children.3, f32[6,128,2048]{2,1,0:T(8,128)} %children.3, f32[6,128,2048]{2,1,0:T(8,128)} %children.3, ...), custom_call_target="tpu_custom_call" | custom-call | tf_op jit(solution)/shard_map/base/pallas_call | solution.py:279
  108.6 0.0 collective-permute-done.12.came
  108.6 0.0 copy-start.2
  108.6 0.9 copy-done.2
  109.5 3.1 %add0.1.old = f32[4,128,1792]{2,1,0:T(8,128)} custom-call(s32[16]{0:T(128)} %get-tuple-element.13.idx, f32[4,128,1792]{2,1,0:T(8,128)} %get-tuple-element.20.old, f32[128,1792]{1,0:T(8,128)} %copy-done.2), custom_call_target="tpu_custom_call", output_to_operand_aliasing={{}: (1, {})} | custom-call | tf_op jit(solution)/shard_map/add0/pallas_call | solution.py:305
  112.7 0.0 collective-permute-done.13.came
  112.7 0.0 copy-start.3
  112.7 0.9 copy-done.3
  113.6 3.1 %add1.1.old = f32[4,128,1792]{2,1,0:T(8,128)} custom-call(s32[16]{0:T(128)} %get-tuple-element.13.idx, f32[4,128,1792]{2,1,0:T(8,128)} %add0.1.old, f32[128,1792]{1,0:T(8,128)} %copy-done.3), custom_call_target="tpu_custom_call", output_to_operand_aliasing={{}: (1, {})} | custom-call | tf_op jit(solution)/shard_map/add1/pallas_call | solution.py:305
  116.7 0.0 collective-permute-done.14.came
  116.7 0.0 copy-start.1
  116.7 0.9 copy-done.1
  117.7 3.1 %add2.1 = f32[4,128,1792]{2,1,0:T(8,128)} custom-call(s32[16]{0:T(128)} %get-tuple-element.13.idx, f32[4,128,1792]{2,1,0:T(8,128)} %add1.1.old, f32[128,1792]{1,0:T(8,128)} %copy-done.1), custom_call_target="tpu_custom_call", output_to_operand_aliasing={{}: (1, {})} | custom-call | tf_op jit(solution)/shard_map/add2/pallas_call | solution.py:305
  (2 shorter events, 0.1 us)
Async XLA Ops:
  4.0 6.9 %collective-permute-start = (f32[128,256]{1,0:T(8,128)}, f32[128,256]{1,0:T(8,128)S(1)}, u32[]{:S(2)}, u32[]{:S(2)}) collective-permute-start(f32[128,256]{1,0:T(8,128)} %get-tuple-element.14), channel_id=1, source_target_pairs={{0,16},{1,17},{2,18},{3,19},{4,20},{5,21},{6,22},{7,23},{8,24},{9,... | collective-permute-start | bytes 393224 | tf_op jit(solution)/shard_map/ppermute | solution.py:338
  10.9 23.3 %copy-start.4 = (f32[128,256]{1,0:T(8,128)}, f32[128,256]{1,0:T(8,128)S(1)}, u32[]{:S(2)}) copy-start(f32[128,256]{1,0:T(8,128)S(1)} %collective-permute-done.refs_10_) | copy-start | bytes 393220
  11.8 7.9 %collective-permute-start.2 = (f32[128,256]{1,0:T(8,128)S(1)}, f32[128,256]{1,0:T(8,128)S(1)}, u32[]{:S(2)}, u32[]{:S(2)}) collective-permute-start(f32[128,256]{1,0:T(8,128)S(1)} %add.4), channel_id=1, source_target_pairs={{0,8},{1,9},{2,10},{3,11},{4,12},{5,13},{6,14},{7,15},{8,0},{9,1},... | collective-permute-start | bytes 393224 | tf_op jit(solution)/shard_map/ppermute | solution.py:338
  15.5 5.3 %collective-permute-start.3 = (f32[128,256]{1,0:T(8,128)S(1)}, f32[128,256]{1,0:T(8,128)S(1)}, u32[]{:S(2)}, u32[]{:S(2)}) collective-permute-start(f32[128,256]{1,0:T(8,128)S(1)} %add.4), channel_id=1, source_target_pairs={{0,16},{1,17},{2,18},{3,19},{4,20},{5,21},{6,22},{7,23},{8,24},{9,... | collective-permute-start | bytes 393224 | tf_op jit(solution)/shard_map/ppermute | solution.py:338
  17.7 5.3 %collective-permute-start.4 = (f32[128,256]{1,0:T(8,128)S(1)}, f32[128,256]{1,0:T(8,128)S(1)}, u32[]{:S(2)}, u32[]{:S(2)}) collective-permute-start(f32[128,256]{1,0:T(8,128)S(1)} %add.4), channel_id=1, source_target_pairs={{0,24},{1,25},{2,26},{3,27},{4,28},{5,29},{6,30},{7,31},{8,16},{9,... | collective-permute-start | bytes 393224 | tf_op jit(solution)/shard_map/ppermute | solution.py:338
  23.0 31.9 %copy-start = (f32[2,128,256]{2,1,0:T(8,128)}, f32[2,128,256]{2,1,0:T(8,128)S(1)}, u32[]{:S(2)}) copy-start(f32[2,128,256]{2,1,0:T(8,128)S(1)} %pad_maximum_fusion.refs_0_) | copy-start | bytes 786436
  23.0 14.8 %collective-permute-start.5 = (f32[2,128,256]{2,1,0:T(8,128)S(1)}, f32[2,128,256]{2,1,0:T(8,128)S(1)}, u32[]{:S(2)}, u32[]{:S(2)}) collective-permute-start(f32[2,128,256]{2,1,0:T(8,128)S(1)} %pad_maximum_fusion.refs_0_), channel_id=1, source_target_pairs={{0,1},{1,0},{2,3},{3,2},{4,5},{5,4},{6,7},{7,6},{8,9},{9,8},{10,11... | collective-permute-start | bytes 786440 | tf_op jit(solution)/shard_map/ppermute | solution.py:338
  23.1 14.7 %collective-permute-start.6 = (f32[2,128,256]{2,1,0:T(8,128)S(1)}, f32[2,128,256]{2,1,0:T(8,128)S(1)}, u32[]{:S(2)}, u32[]{:S(2)}) collective-permute-start(f32[2,128,256]{2,1,0:T(8,128)S(1)} %pad_maximum_fusion.refs_0_), channel_id=1, source_target_pairs={{0,6},{1,7},{2,0},{3,1},{4,2},{5,3},{6,4},{7,5},{8,14},{9,15},{10,... | collective-permute-start | bytes 786440 | tf_op jit(solution)/shard_map/ppermute | solution.py:338
  27.3 81.3 %collective-permute-start.12 = (f32[128,1792]{1,0:T(8,128)}, f32[128,1792]{1,0:T(8,128)S(1)}, u32[]{:S(2)}, u32[]{:S(2)}) collective-permute-start(f32[128,1792]{1,0:T(8,128)} %get-tuple-element.21), channel_id=1, source_target_pairs={{0,16},{1,17},{2,18},{3,19},{4,20},{5,21},{6,22},{7,23},{8,24},{9,... | collective-permute-start | bytes 2752520 | tf_op jit(solution)/shard_map/ppermute | solution.py:338
  34.2 78.4 %collective-permute-start.13 = (f32[128,1792]{1,0:T(8,128)}, f32[128,1792]{1,0:T(8,128)S(1)}, u32[]{:S(2)}, u32[]{:S(2)}) collective-permute-start(f32[128,1792]{1,0:T(8,128)} %get-tuple-element.22), channel_id=1, source_target_pairs={{0,16},{1,17},{2,18},{3,19},{4,20},{5,21},{6,22},{7,23},{8,24},{9,... | collective-permute-start | bytes 2752520 | tf_op jit(solution)/shard_map/ppermute | solution.py:338
  34.3 82.4 %collective-permute-start.14 = (f32[128,1792]{1,0:T(8,128)}, f32[128,1792]{1,0:T(8,128)S(1)}, u32[]{:S(2)}, u32[]{:S(2)}) collective-permute-start(f32[128,1792]{1,0:T(8,128)} %get-tuple-element.23), channel_id=1, source_target_pairs={{0,16},{1,17},{2,18},{3,19},{4,20},{5,21},{6,22},{7,23},{8,24},{9,... | collective-permute-start | bytes 2752520 | tf_op jit(solution)/shard_map/ppermute | solution.py:338
  37.8 17.1 %copy-start.6 = (f32[2,128,256]{2,1,0:T(8,128)}, f32[2,128,256]{2,1,0:T(8,128)S(1)}, u32[]{:S(2)}) copy-start(f32[2,128,256]{2,1,0:T(8,128)S(1)} %collective-permute-done.5.refs_1_) | copy-start | bytes 786436
  37.8 10.7 %collective-permute-start.8 = (f32[2,128,256]{2,1,0:T(8,128)S(1)}, f32[2,128,256]{2,1,0:T(8,128)S(1)}, u32[]{:S(2)}, u32[]{:S(2)}) collective-permute-start(f32[2,128,256]{2,1,0:T(8,128)S(1)} %pad_maximum_fusion.refs_0_), channel_id=1, source_target_pairs={{0,4},{1,5},{2,6},{3,7},{4,0},{5,1},{6,2},{7,3},{8,12},{9,13},{10,... | collective-permute-start | bytes 786440 | tf_op jit(solution)/shard_map/ppermute | solution.py:338
  37.8 17.1 %copy-start.7 = (f32[2,128,256]{2,1,0:T(8,128)}, f32[2,128,256]{2,1,0:T(8,128)S(1)}, u32[]{:S(2)}) copy-start(f32[2,128,256]{2,1,0:T(8,128)S(1)} %collective-permute-done.6.refs_2_) | copy-start | bytes 786436
  37.8 14.4 %collective-permute-start.10 = (f32[2,128,256]{2,1,0:T(8,128)S(1)}, f32[2,128,256]{2,1,0:T(8,128)S(1)}, u32[]{:S(2)}, u32[]{:S(2)}) collective-permute-start(f32[2,128,256]{2,1,0:T(8,128)S(1)} %pad_maximum_fusion.refs_0_), channel_id=1, source_target_pairs={{0,2},{1,3},{2,4},{3,5},{4,6},{5,7},{6,0},{7,1},{8,10},{9,11},{10,... | collective-permute-start | bytes 786440 | tf_op jit(solution)/shard_map/ppermute | solution.py:338
  48.6 6.3 %copy-start.8 = (f32[2,128,256]{2,1,0:T(8,128)}, f32[2,128,256]{2,1,0:T(8,128)S(1)}, u32[]{:S(2)}) copy-start(f32[2,128,256]{2,1,0:T(8,128)S(1)} %collective-permute-done.8.refs_4_) | copy-start | bytes 786436
  48.6 3.7 %collective-permute-start.7 = (f32[2,128,256]{2,1,0:T(8,128)S(1)}, f32[2,128,256]{2,1,0:T(8,128)S(1)}, u32[]{:S(2)}, u32[]{:S(2)}) collective-permute-start(f32[2,128,256]{2,1,0:T(8,128)S(1)} %collective-permute-done.6.refs_2_), channel_id=1, source_target_pairs={{0,1},{1,0},{2,3},{3,2},{4,5},{5,4},{6,7},{7,6},{8,9},{9,8},{10,11... | collective-permute-start | bytes 786440 | tf_op jit(solution)/shard_map/ppermute | solution.py:338
  52.3 1.5 %copy-start.9 = (f32[2,128,256]{2,1,0:T(8,128)}, f32[2,128,256]{2,1,0:T(8,128)S(1)}, u32[]{:S(2)}) copy-start(f32[2,128,256]{2,1,0:T(8,128)S(1)} %collective-permute-done.10.refs_6_) | copy-start | bytes 786436
  52.3 1.5 %collective-permute-start.9 = (f32[2,128,256]{2,1,0:T(8,128)S(1)}, f32[2,128,256]{2,1,0:T(8,128)S(1)}, u32[]{:S(2)}, u32[]{:S(2)}) collective-permute-start(f32[2,128,256]{2,1,0:T(8,128)S(1)} %collective-permute-done.8.refs_4_), channel_id=1, source_target_pairs={{0,1},{1,0},{2,3},{3,2},{4,5},{5,4},{6,7},{7,6},{8,9},{9,8},{10,11... | collective-permute-start | bytes 786440 | tf_op jit(solution)/shard_map/ppermute | solution.py:338
  52.3 1.5 %copy-start.10 = (f32[2,128,256]{2,1,0:T(8,128)}, f32[2,128,256]{2,1,0:T(8,128)S(1)}, u32[]{:S(2)}) copy-start(f32[2,128,256]{2,1,0:T(8,128)S(1)} %collective-permute-done.7.refs_3_) | copy-start | bytes 786436
  52.3 2.6 %collective-permute-start.11 = (f32[2,128,256]{2,1,0:T(8,128)S(1)}, f32[2,128,256]{2,1,0:T(8,128)}, u32[]{:S(2)}, u32[]{:S(2)}) collective-permute-start(f32[2,128,256]{2,1,0:T(8,128)S(1)} %collective-permute-done.10.refs_6_), channel_id=1, source_target_pairs={{0,1},{1,0},{2,3},{3,2},{4,5},{5,4},{6,7},{7,6},{8,9},{9,8},{10,11... | collective-permute-start | bytes 786440 | tf_op jit(solution)/shard_map/ppermute | solution.py:338
  53.8 0.7 copy-start.11
  54.5 42.1 %collective-permute-start.1 = (f32[2,128,256]{2,1,0:T(8,128)}, f32[2,128,256]{2,1,0:T(8,128)S(1)}, u32[]{:S(2)}, u32[]{:S(2)}) collective-permute-start(f32[2,128,256]{2,1,0:T(8,128)} %get-tuple-element.15), channel_id=1, source_target_pairs={{0,16},{1,17},{2,18},{3,19},{4,20},{5,21},{6,22},{7,23},{8,24},{9,... | collective-permute-start | bytes 786440 | tf_op jit(solution)/shard_map/ppermute | solution.py:338
  96.6 0.7 copy-start.5
  108.6 0.9 copy-start.2
  112.7 0.9 copy-start.3
  116.7 0.9 copy-start.1

commit v2 on v1

--- a/solution.py
+++ b/solution.py
@@ -9,9 +9,12 @@
 
 PANEL = 256
 BLK = 128
+LANES = 128
 HIGHEST = lax.Precision.HIGHEST
 VMEM_LIMIT = 60 << 20
 GROUP = 64
+HEAD = 1152
+CHUNKS = ((0, 0, HEAD), (1, 256, 1792), (2, 256, 1792), (0, HEAD, 896))
 
 OUT = 0
 SLOT = 4
@@ -26,6 +29,14 @@
     )
 
 
+def split(a):
+    parts = []
+    for _ in range(3):
+        parts.append(a.astype(jnp.bfloat16))
+        a = a - parts[-1].astype(jnp.float32)
+    return parts
+
+
 def any_space():
     return pl.BlockSpec(memory_space=pl.ANY)
 
@@ -38,9 +49,7 @@
     return pltpu.CompilerParams(vmem_limit_bytes=VMEM_LIMIT)
 
 
-def index_kernel(
-    half, slots, maps, front, children, idx, piece, rest, others, base, mine, theirs, old, kept, sem
-):
+def index_kernel(half, slots, maps, front, children, idx, piece, others, mine, theirs, old, kept, sent, sem):
     dev = lax.axis_index("sub")
     sib = dev // half
     res = dev % half
@@ -71,24 +80,21 @@
     idx[SLOT + 3] = none
     keep = idx[KEEP]
     copies = [
-        pltpu.make_async_copy(children.at[idx[OUT], :, lead], piece, sem.at[1]),
-        pltpu.make_async_copy(children.at[jnp.maximum(keep, 0), :, lead], kept, sem.at[2]),
-        pltpu.make_async_copy(
-            children.at[idx[OUT], :, pl.ds(PANEL, rest.shape[1])], rest, sem.at[3]
-        ),
-        pltpu.make_async_copy(children.at[idx[OUT + 1], :, lead], others.at[0], sem.at[4]),
-        pltpu.make_async_copy(children.at[idx[OUT + 2], :, lead], others.at[1], sem.at[5]),
+        pltpu.make_async_copy(children.at[jnp.maximum(keep, 0), :, lead], kept, sem.at[1])
+    ] + [
+        pltpu.make_async_copy(children.at[idx[OUT + i], :, lead], out, sem.at[2 + i])
+        for i, out in enumerate((sent, others.at[0], others.at[1]))
     ]
     for copy in copies:
         copy.start()
     first.wait()
     for copy in copies:
         copy.wait()
-    base[...] = old[...] + kept[...] * jnp.where(keep >= 0, 1.0, 0.0)
+    mine_at_0 = old[...] + kept[...] * jnp.where(keep >= 0, 1.0, 0.0)
+    piece[...] = jnp.where(sib == 0, mine_at_0, sent[...])
 
 
 def make_indices(row_maps, front, children, half):
-    rest = children.shape[2] - PANEL
     vmem = pl.BlockSpec(memory_space=pltpu.VMEM)
     return pl.pallas_call(
         functools.partial(index_kernel, half, children.shape[0]),
@@ -96,30 +102,29 @@
         out_shape=(
             jax.ShapeDtypeStruct((16,), jnp.int32),
             jax.ShapeDtypeStruct((BLK, PANEL), jnp.float32),
-            jax.ShapeDtypeStruct((BLK, rest), jnp.float32),
             jax.ShapeDtypeStruct((2, BLK, PANEL), jnp.float32),
-            jax.ShapeDtypeStruct((BLK, PANEL), jnp.float32),
         ),
         in_specs=[smem_space(), any_space(), any_space()],
-        out_specs=(smem_space(), vmem, vmem, vmem, vmem),
+        out_specs=(smem_space(), vmem, vmem),
         scratch_shapes=[
             pltpu.SMEM((8,), jnp.int32),
             pltpu.SMEM((8,), jnp.int32),
             pltpu.VMEM((BLK, PANEL), jnp.float32),
             pltpu.VMEM((BLK, PANEL), jnp.float32),
-            pltpu.SemaphoreType.DMA((6,)),
+            pltpu.VMEM((BLK, PANEL), jnp.float32),
+            pltpu.SemaphoreType.DMA((5,)),
         ],
         compiler_params=params(),
         cost_estimate=SMALL,
     )(row_maps, front, children)
 
 
-def take_kernel(idx, children, one, two, sem):
-    part = pl.ds(PANEL, one.shape[1])
-    copies = [
-        pltpu.make_async_copy(children.at[idx[OUT + 1 + i], :, part], out, sem.at[i])
-        for i, out in enumerate((one, two))
-    ]
+def take_kernel(idx, children, *refs):
+    outs, sem = refs[:-1], refs[-1]
+    copies = []
+    for i, (out, (which, low, width)) in enumerate(zip(outs, CHUNKS)):
+        part = pl.ds(low, width)
+        copies.append(pltpu.make_async_copy(children.at[idx[OUT + which], :, part], out, sem.at[i]))
     for copy in copies:
         copy.start()
     for copy in copies:
@@ -127,18 +132,56 @@
 
 
 def take_blocks(idx, children):
-    shape = jax.ShapeDtypeStruct((BLK, children.shape[2] - PANEL), jnp.float32)
     vmem = pl.BlockSpec(memory_space=pltpu.VMEM)
     return pl.pallas_call(
         take_kernel,
         name="take",
-        out_shape=(shape, shape),
+        out_shape=[jax.ShapeDtypeStruct((BLK, width), jnp.float32) for _, _, width in CHUNKS],
         in_specs=[smem_space(), any_space()],
-        out_specs=(vmem, vmem),
-        scratch_shapes=[pltpu.SemaphoreType.DMA((2,))],
+        out_specs=[vmem for _ in CHUNKS],
+        scratch_shapes=[pltpu.SemaphoreType.DMA((len(CHUNKS),))],
         compiler_params=params(),
         cost_estimate=SMALL,
     )(idx, children)
+
+
+def lead_kernel(n, *refs):
+    refs[2 + n][...] = refs[0][...] + refs[1][...]
+
+
+def lead_piece(piece, came, later):
+    vmem = pl.BlockSpec(memory_space=pltpu.VMEM)
+    n = len(later)
+    out = pl.pallas_call(
+        functools.partial(lead_kernel, n),
+        name="lead",
+        out_shape=[jax.ShapeDtypeStruct((BLK, PANEL), jnp.float32)]
+        + [jax.ShapeDtypeStruct(b.shape, b.dtype) for b in later],
+        in_specs=[vmem, vmem] + [any_space() for _ in later],
+        out_specs=[vmem] + [any_space() for _ in later],
+        input_output_aliases={2 + i: 1 + i for i in range(n)},
+        compiler_params=params(),
+        cost_estimate=SMALL,
+    )(piece, came, *later)
+    return out[0], list(out[1:])
+
+
+def pair_kernel(*refs):
+    refs[-1][0] = refs[0][...]
+    refs[-1][1] = refs[1][...]
+
+
+def pair(one, two, *after):
+    vmem = pl.BlockSpec(memory_space=pltpu.VMEM)
+    return pl.pallas_call(
+        pair_kernel,
+        name="pair",
+        out_shape=jax.ShapeDtypeStruct((2, BLK, PANEL), jnp.float32),
+        in_specs=[vmem] * 2 + [any_space() for _ in after],
+        out_specs=vmem,
+        compiler_params=params(),
+        cost_estimate=SMALL,
+    )(one, two, *after)
 
 
 def inverse_factor(d):
@@ -174,15 +217,16 @@
 
 
 def factor_kernel(half, *refs):
-    pieces, (inv, wide), (window, m) = refs[:8], refs[8:10], refs[10:]
+    pieces, (inv, wide, window, m) = refs[:8], refs[-4:]
     dev = lax.axis_index("sub")
+    h0 = (dev // 8) % 2
     z = (dev // 2) % 4
     core = dev % 2
     for i, ref in enumerate(pieces):
         zz = (z + i // 2) % 4
         cc = (core + i) % 2
         for h in range(2):
-            block = (h * 4 + zz) * 2 + cc
+            block = ((h0 + h) % 2 * 4 + zz) * 2 + cc
             window[pl.ds(pl.multiple_of(block * BLK, BLK), BLK), :] = ref[h]
     s = window[0:PANEL, :]
     s = 0.5 * (s + s.T)
@@ -199,29 +243,30 @@
             m[b:, :] = m[b:, :] - matmul(x[:, b:PANEL], x, 0, 0)
     linv = m[:, PANEL:]
     inv[...] = linv
-    wide[...] = matmul(window[PANEL:, :], linv, 1, 1)
-
-
-def factor(pieces, half, columns):
+    wide[...] = jnp.concatenate(split(matmul(window[PANEL:, :], linv, 1, 1)), axis=1)
+
+
+def factor(pieces, half, columns, *after):
     return pl.pallas_call(
         functools.partial(factor_kernel, half),
         name="factor",
         out_shape=(
             jax.ShapeDtypeStruct((PANEL, PANEL), jnp.float32),
-            jax.ShapeDtypeStruct((columns - PANEL, PANEL), jnp.float32),
+            jax.ShapeDtypeStruct((columns - PANEL, 3 * PANEL), jnp.bfloat16),
         ),
+        in_specs=[pl.BlockSpec(memory_space=pltpu.VMEM)] * 8 + [any_space() for _ in after],
         scratch_shapes=[
             pltpu.VMEM((columns, PANEL), jnp.float32),
             pltpu.VMEM((PANEL, 2 * PANEL), jnp.float32),
         ],
         compiler_params=params(),
         cost_estimate=SMALL,
-    )(*pieces)
+    )(*pieces, *after)
 
 
 def base_kernel(slots, idx, *refs):
-    fronts, (lead_front,), refs = refs[:1], refs[1:2], refs[2:]
-    kept, lead_kept, (came, others, inv, wide, panel, update, held) = (
+    fronts, lead_front, refs = refs[0], refs[1], refs[2:]
+    kept, lead_kept, (others, head, inv, wide, *_, panel, update, held) = (
         refs[:slots], refs[slots : 2 * slots], refs[2 * slots :]
     )
     has = [jnp.where(idx[KEEP + q] >= 0, 1.0, 0.0) for q in range(slots)]
@@ -230,22 +275,35 @@
     def _():
         for q in range(slots):
             which = idx[CAME + q]
-            second = others[jnp.clip(which - 1, 0, 1)]
-            got = jnp.where(which == 0, came[...], jnp.where(which > 0, second, 0.0))
-            held[q * BLK : (q + 1) * BLK, :] = (
-                lead_front[q] + lead_kept[q][0] * has[q] + got
-            )
-        p = matmul(held[...], inv[...], 1, 1)
-        held[...] = p
-        for q in range(slots):
-            panel[q] = p[q * BLK : (q + 1) * BLK, :]
-
-    u = matmul(held[...], wide[...], 1, 1)
+            second = others[jnp.clip(which - 1, 0, 1)] * jnp.where(which >= 0, 1.0, 0.0)
+            got = jnp.where(which == 0, head[:, :PANEL], second)
+            panel[q] = lead_front[q] + lead_kept[q][0] * has[q] + got
+        p = matmul(panel[...].reshape(slots * BLK, PANEL), inv[...], 1, 1)
+        panel[...] = p.reshape(slots, BLK, PANEL)
+        a, b, c = split(p)
+        for i, part in enumerate((a, a, b, b, a, c)):
+            held[:, i * PANEL : (i + 1) * PANEL] = part
+
+    def block0(part):
+        at = PANEL + pl.program_id(0) * PANEL + part * LANES
+        first = pl.multiple_of(jnp.minimum(at, HEAD - LANES), LANES)
+        return head[:, pl.ds(first, LANES)] * jnp.where(at < HEAD, 1.0, 0.0)
+
+    a, b, c = (wide[:, i * PANEL : (i + 1) * PANEL] for i in range(3))
+    u = lax.dot_general(
+        held[...],
+        jnp.concatenate([a, b, a, b, c, a], axis=1),
+        (((1,), (1,)), ((), ())),
+        preferred_element_type=jnp.float32,
+    )
     for q in range(slots):
-        update[q] = fronts[0][q] + kept[q][0] * has[q] - u[q * BLK : (q + 1) * BLK, :]
-
-
-def make_base(idx, front, children, came, others, inv, wide):
+        new = fronts[q] + kept[q][0] * has[q] - u[q * BLK : (q + 1) * BLK, :]
+        if q == 0:
+            new = new + jnp.concatenate([block0(0), block0(1)], axis=1)
+        update[q] = new
+
+
+def make_base(idx, front, children, others, head, inv, wide, *after):
     slots, rows, columns = front.shape
     rest = columns - PANEL
     whole = lambda shape: pl.BlockSpec(shape, lambda i, idx: (0,) * len(shape))
@@ -260,11 +318,12 @@
         + [kept(q, 1) for q in range(slots)]
         + [kept(q, 0) for q in range(slots)]
         + [
-            whole(came.shape),
             whole(others.shape),
+            whole(head.shape),
             whole(inv.shape),
-            pl.BlockSpec((PANEL, PANEL), lambda i, idx: (i, 0)),
+            pl.BlockSpec((PANEL, 3 * PANEL), lambda i, idx: (i, 0)),
         ]
+        + [any_space() for _ in after]
     )
     grid = pltpu.PrefetchScalarGridSpec(
         num_scalar_prefetch=1,
@@ -274,7 +333,7 @@
             whole((slots, rows, PANEL)),
             pl.BlockSpec((slots, rows, PANEL), lambda i, idx: (0, 0, i)),
         ),
-        scratch_shapes=[pltpu.VMEM((slots * rows, PANEL), jnp.float32)],
+        scratch_shapes=[pltpu.VMEM((slots * rows, 6 * PANEL), jnp.bfloat16)],
     )
     return pl.pallas_call(
         functools.partial(base_kernel, slots),
@@ -286,7 +345,7 @@
         grid_spec=grid,
         compiler_params=params(),
         cost_estimate=SMALL,
-    )(idx, *[front] * 2, *[children] * (2 * slots), came, others, inv, wide)
+    )(idx, *[front] * 2, *[children] * (2 * slots), others, head, inv, wide, *after)
 
 
 def add_kernel(idx, old, came, out):
@@ -295,7 +354,10 @@
 
 def add_block(idx, update, came, which):
     slots, rows, rest = update.shape
-    at_slot = pl.BlockSpec((1, rows, rest), lambda i, idx: (idx[SLOT + which], 0, 0))
+    block, low, width = CHUNKS[which]
+    at_slot = pl.BlockSpec(
+        (1, rows, width), lambda i, idx: (idx[SLOT + block], 0, (low - PANEL) // width)
+    )
     grid = pltpu.PrefetchScalarGridSpec(
         num_scalar_prefetch=1,
         grid=(1,),
@@ -325,9 +387,7 @@
 
 
 OPPOSITE = route(lambda x, z, c: ((x + 2) % 4, z, c))
-SIDE = route(lambda x, z, c: (1 - x, z, c), lambda x: x < 2)
-BACK = route(lambda x, z, c: (3 - x, z, c), lambda x: x < 2)
-ACROSS = route(lambda x, z, c: (x + 2, z, c), lambda x: x < 2)
+SIDE = route(lambda x, z, c: (x ^ 1, z, c))
 Z_UP = route(lambda x, z, c: (x, (z + 1) % 4, c))
 Z_DOWN = route(lambda x, z, c: (x, (z + 3) % 4, c))
 Z_FAR = route(lambda x, z, c: (x, (z + 2) % 4, c))
@@ -341,29 +401,26 @@
 def per_device(front, children, row_maps):
     half = lax.axis_size("sub") // 2
     columns = front.shape[2]
-    x = lax.axis_index("sub") // 8
-
-    idx, first, b0, second, base_lead = make_indices(row_maps, front, children, half)
-    came_first = send(first, OPPOSITE)
-    came_others = send(second, OPPOSITE)
-    b1, b2 = take_blocks(idx, children)
-    came = [send(b, OPPOSITE) for b in (b0, b1, b2)]
-
-    lead = base_lead + came_first
-    side, back, across = send(lead, SIDE), send(lead, BACK), send(lead, ACROSS)
-    row_a = jnp.where(x == 0, lead, jnp.where(x == 1, side, jnp.where(x == 2, across, back)))
-    row_b = jnp.where(x == 1, lead, jnp.where(x == 0, side, jnp.where(x == 3, across, back)))
-    own = jnp.stack([row_a, row_b])
+
+    idx, piece, panels = make_indices(row_maps, front, children, half)
+    came_piece = send(piece, OPPOSITE)
+    blocks = take_blocks(idx, children)
+    came_panels = send(panels, OPPOSITE)
+
+    lead, blocks = lead_piece(piece, came_piece, blocks)
+    came = [send(b, OPPOSITE) for b in blocks]
+    own = pair(lead, send(lead, SIDE), came_panels)
 
     by_z = [own, send(own, Z_DOWN), send(own, Z_FAR), send(own, Z_UP)]
+    *by_z, came[0] = lax.optimization_barrier((*by_z, came[0]))
     pieces = []
     for v in by_z:
         pieces += [v, send(v, CORE)]
     inv, wide = factor(pieces, half, columns)
 
-    panel, update = make_base(idx, front, children, came_first, came_others, inv, wide)
-    for which, block in enumerate(came):
-        update = add_block(idx, update, block, which)
+    panel, update = make_base(idx, front, children, came_panels, came[0], inv, wide)
+    for which in range(1, len(CHUNKS)):
+        update = add_block(idx, update, came[which], which)
     return panel, update
 
 

time: 122 us -> 86.1 us (0.71)
  waiting for transfers between devices: 49.5 us -> 10.1 us
  Pallas kernels: 41.5 us -> 44.9 us
  starting transfers between devices: 23.8 us -> 25.2 us
    ppermute x15 -> x14, waiting for transfers between devices: 49.5 us -> 10.1 us  [send(): return lax.ppermute(value, 'sub', pairs)]
    pallas_call x1 -> x3, Pallas kernels: 3.38 us -> 7.33 us  [the longest x1 4.01 us: take_blocks(): pl.pallas_call(take_kernel, name='take', out_shape=[jax.ShapeDtypeStruct(...]
    ppermute x15 -> x14, starting transfers between devices: 23.8 us -> 25.2 us  [send(): return lax.ppermute(value, 'sub', pairs)]
    unnamed x24 -> x26, local copies, waits for them, and re-layouts: 4.23 us -> 4.64 us
  transfers between devices with their start and end apart: 15 -> 14, of which waited for: 8 -> 6; matrix products, arithmetic and copies ran while one was open for 0% -> 0% of each run, Pallas kernels for 29% -> 46%
where the time goes in v2:
time: 86.1 us; the launch traced here: 85.6 us
  Pallas kernels  44.9 us (52%)
  starting transfers between devices  25.2 us (29%)
  waiting for transfers between devices  10.1 us (12%)
  local copies, waits for them, and re-layouts  4.64 us (5%)
    ppermute x14, starting transfers between devices, send(): return lax.ppermute(value, 'sub', pairs)  25.2 us
    pallas_call x1, Pallas kernels, factor(): pl.pallas_call(functools.partial(factor_kernel, half), name='factor', out...  14.5 us
    pallas_call x1, Pallas kernels, make_base(): pl.pallas_call(functools.partial(base_kernel, slots), name='base', out_sh...  11.5 us
    ppermute x14, waiting for transfers between devices, send(): return lax.ppermute(value, 'sub', pairs)  10.1 us
    pallas_call x3, Pallas kernels, add_block(): pl.pallas_call(add_kernel, name=f'add{which}', out_shape=jax.ShapeDtypeSt...  8.9 us
    unnamed x26, local copies, waits for them, and re-layouts  4.64 us
    pallas_call x1, Pallas kernels, take_blocks(): pl.pallas_call(take_kernel, name='take', out_shape=[jax.ShapeDtypeStruct(...  4.01 us
    pallas_call x1, Pallas kernels, make_indices(): pl.pallas_call(functools.partial(index_kernel, half, children.shape[0]),...  2.67 us
  transfers between devices with their start and end apart: 14, of which 6 were waited for; matrix products, arithmetic and copies ran while one was open for 0% of the time, Pallas kernels for 46%

profile of v2, /device:TPU:0, one launch (start us, length us, event | category | flops | bytes accessed | tf_op | source)
XLA Modules:
  0.0 85.6 jit_solution(12568783444677222002)
XLA Ops:
  0.6 2.7 %indices.1 = (s32[16]{0:T(128)}, f32[128,256]{1,0:T(8,128)}, f32[2,128,256]{2,1,0:T(8,128)}) custom-call(s32[2,96]{1,0:T(2,128)} %maps.1, f32[4,128,2048]{2,1,0:T(8,128)} %refs_1_.1, f32[6,128,2048]{2,1,0:T(8,128)} %refs_9_.1), custom_call_target="tpu_custom_call" | custom-call | tf_op jit(solution)/shard_map/indices/pallas_call | solution.py:99
  3.3 3.2 %collective-permute-start.1 = (f32[128,256]{1,0:T(8,128)}, f32[128,256]{1,0:T(8,128)S(1)}, u32[]{:S(2)}, u32[]{:S(2)}) collective-permute-start(f32[128,256]{1,0:T(8,128)} %get-tuple-element.25.refs_0_), channel_id=1, source_target_pairs={{0,16},{1,17},{2,18},{3,19},{4,20},{5,21},{6,22},{7,23},{8,24},{9,... | collective-permute-start | bytes 393224 | tf_op jit(solution)/shard_map/ppermute | solution.py:398
  6.5 0.4 collective-permute-start
  6.9 4.0 %take.1 = (f32[128,1152]{1,0:T(8,128)}, f32[128,1792]{1,0:T(8,128)}, f32[128,1792]{1,0:T(8,128)}, f32[128,896]{1,0:T(8,128)}) custom-call(s32[16]{0:T(128)} %get-tuple-element.23.idx, f32[6,128,2048]{2,1,0:T(8,128)} %refs_9_.1), custom_call_target="tpu_custom_call" | custom-call | tf_op jit(solution)/shard_map/take/pallas_call | solution.py:136
  10.9 0.0 collective-permute-done.1.refs_1_
  10.9 0.0 copy-start.11
  11.0 0.6 copy-done.11
  11.6 1.6 %lead.1 = (f32[128,256]{1,0:T(8,128)}, f32[128,1152]{1,0:T(8,128)}, f32[128,1792]{1,0:T(8,128)}, f32[128,1792]{1,0:T(8,128)}, f32[128,896]{1,0:T(8,128)}) custom-call(f32[128,256]{1,0:T(8,128)} %get-tuple-element.25.refs_0_, f32[128,256]{1,0:T(8,128)} %copy-done.11, ...), custom_call_target="tpu_custom_call", output_to_operand_aliasing={{1}: (2, {}), {2}: (3, {}), {3}: (4, {}), {4}: (5, {})} | custom-call | tf_op jit(solution)/shard_map/lead/pallas_call | solution.py:155
  13.2 2.0 %collective-permute-start.2 = (f32[128,256]{1,0:T(8,128)}, f32[128,256]{1,0:T(8,128)S(1)}, u32[]{:S(2)}, u32[]{:S(2)}) collective-permute-start(f32[128,256]{1,0:T(8,128)} %get-tuple-element.30.refs_0_), channel_id=1, source_target_pairs={{0,8},{1,9},{2,10},{3,11},{4,12},{5,13},{6,14},{7,15},{8,0},{9,1},... | collective-permute-start | bytes 393224 | tf_op jit(solution)/shard_map/ppermute | solution.py:398
  15.2 2.9 %collective-permute-start.6 = (f32[128,1152]{1,0:T(8,128)}, f32[128,1152]{1,0:T(8,128)S(1)}, u32[]{:S(2)}, u32[]{:S(2)}) collective-permute-start(f32[128,1152]{1,0:T(8,128)} %get-tuple-element.31), channel_id=1, source_target_pairs={{0,16},{1,17},{2,18},{3,19},{4,20},{5,21},{6,22},{7,23},{8,24},{9,... | collective-permute-start | bytes 1769480 | tf_op jit(solution)/shard_map/ppermute | solution.py:398
  18.1 0.0 collective-permute-done.refs_2_.refs_10_
  18.1 0.0 copy-start
  18.1 1.8 %collective-permute-done.2.refs_1_ = f32[128,256]{1,0:T(8,128)S(1)} collective-permute-done((f32[128,256]{1,0:T(8,128)}, f32[128,256]{1,0:T(8,128)S(1)}, u32[]{:S(2)}, u32[]{:S(2)}) %collective-permute-start.2) | collective-permute-done | bytes 131104 | tf_op jit(solution)/shard_map/ppermute | solution.py:398
  19.9 0.0 copy-done
  19.9 0.0 copy-start.12
  19.9 0.6 copy-done.12
  20.5 1.7 %pair.1.refs_0_ = f32[2,128,256]{2,1,0:T(8,128)} custom-call(f32[128,256]{1,0:T(8,128)} %get-tuple-element.30.refs_0_, f32[128,256]{1,0:T(8,128)} %copy-done.12, f32[2,128,256]{2,1,0:T(8,128)} %copy-done), custom_call_target="tpu_custom_call" | custom-call | tf_op jit(solution)/shard_map/pair/pallas_call | solution.py:176
  22.2 2.0 %collective-permute-start.5 = (f32[2,128,256]{2,1,0:T(8,128)}, f32[2,128,256]{2,1,0:T(8,128)S(1)}, u32[]{:S(2)}, u32[]{:S(2)}) collective-permute-start(f32[2,128,256]{2,1,0:T(8,128)} %pair.1.refs_0_), channel_id=1, source_target_pairs={{0,2},{1,3},{2,4},{3,5},{4,6},{5,7},{6,0},{7,1},{8,10},{9,11},{10,... | collective-permute-start | bytes 786440 | tf_op jit(solution)/shard_map/ppermute | solution.py:398
  24.2 3.6 %collective-permute-start.11 = (f32[128,1792]{1,0:T(8,128)}, f32[128,1792]{1,0:T(8,128)S(1)}, u32[]{:S(2)}, u32[]{:S(2)}) collective-permute-start(f32[128,1792]{1,0:T(8,128)} %get-tuple-element.41), channel_id=1, source_target_pairs={{0,16},{1,17},{2,18},{3,19},{4,20},{5,21},{6,22},{7,23},{8,24},{9,... | collective-permute-start | bytes 2752520 | tf_op jit(solution)/shard_map/ppermute | solution.py:398
  27.8 0.0 collective-permute-start.12
  27.8 3.6 %collective-permute-start.4 = (f32[2,128,256]{2,1,0:T(8,128)}, f32[2,128,256]{2,1,0:T(8,128)S(1)}, u32[]{:S(2)}, u32[]{:S(2)}) collective-permute-start(f32[2,128,256]{2,1,0:T(8,128)} %pair.1.refs_0_), channel_id=1, source_target_pairs={{0,4},{1,5},{2,6},{3,7},{4,0},{5,1},{6,2},{7,3},{8,12},{9,13},{10,... | collective-permute-start | bytes 786440 | tf_op jit(solution)/shard_map/ppermute | solution.py:398
  31.4 1.1 %collective-permute-done.5.refs_6_ = f32[2,128,256]{2,1,0:T(8,128)S(1)} collective-permute-done((f32[2,128,256]{2,1,0:T(8,128)}, f32[2,128,256]{2,1,0:T(8,128)S(1)}, u32[]{:S(2)}, u32[]{:S(2)}) %collective-permute-start.5) | collective-permute-done | bytes 262176 | tf_op jit(solution)/shard_map/ppermute | solution.py:398
  32.5 0.0 copy-start.5
  32.5 3.2 %collective-permute-start.3 = (f32[2,128,256]{2,1,0:T(8,128)}, f32[2,128,256]{2,1,0:T(8,128)S(1)}, u32[]{:S(2)}, u32[]{:S(2)}) collective-permute-start(f32[2,128,256]{2,1,0:T(8,128)} %pair.1.refs_0_), channel_id=1, source_target_pairs={{0,6},{1,7},{2,0},{3,1},{4,2},{5,3},{6,4},{7,5},{8,14},{9,15},{10,... | collective-permute-start | bytes 786440 | tf_op jit(solution)/shard_map/ppermute | solution.py:398
  35.7 2.3 %collective-permute-done.4.refs_4_ = f32[2,128,256]{2,1,0:T(8,128)S(1)} collective-permute-done((f32[2,128,256]{2,1,0:T(8,128)}, f32[2,128,256]{2,1,0:T(8,128)S(1)}, u32[]{:S(2)}, u32[]{:S(2)}) %collective-permute-start.4) | collective-permute-done | bytes 262176 | tf_op jit(solution)/shard_map/ppermute | solution.py:398
  38.0 0.0 copy-start.6
  38.0 2.3 %collective-permute-done.3.refs_2_ = f32[2,128,256]{2,1,0:T(8,128)S(1)} collective-permute-done((f32[2,128,256]{2,1,0:T(8,128)}, f32[2,128,256]{2,1,0:T(8,128)S(1)}, u32[]{:S(2)}, u32[]{:S(2)}) %collective-permute-start.3) | collective-permute-done | bytes 262176 | tf_op jit(solution)/shard_map/ppermute | solution.py:398
  40.2 0.0 copy-start.7
  40.2 0.0 collective-permute-done.6.refs_11_
  40.2 0.0 copy-start.3
  40.2 0.1 collective-permute-start.7
  40.3 0.5 collective-permute-start.8
  40.8 3.3 %collective-permute-start.13 = (f32[128,896]{1,0:T(8,128)}, f32[128,896]{1,0:T(8,128)S(1)}, u32[]{:S(2)}, u32[]{:S(2)}) collective-permute-start(f32[128,896]{1,0:T(8,128)} %get-tuple-element.43), channel_id=1, source_target_pairs={{0,16},{1,17},{2,18},{3,19},{4,20},{5,21},{6,22},{7,23},{8,24},{9,... | collective-permute-start | bytes 1376264 | tf_op jit(solution)/shard_map/ppermute | solution.py:398
  44.2 0.0 collective-permute-done.7.refs_1_
  44.2 0.0 copy-start.8
  44.2 0.0 collective-permute-start.9
  44.2 0.0 collective-permute-done.8.refs_3_
  44.2 0.0 copy-start.9
  44.2 0.5 collective-permute-start.10
  44.7 1.0 %collective-permute-done.9.refs_5_ = f32[2,128,256]{2,1,0:T(8,128)S(1)} collective-permute-done((f32[2,128,256]{2,1,0:T(8,128)S(1)}, f32[2,128,256]{2,1,0:T(8,128)S(1)}, u32[]{:S(2)}, u32[]{:S(2)}) %collective-permute-start.9) | collective-permute-done | bytes 262176 | tf_op jit(solution)/shard_map/ppermute | solution.py:398
  45.7 0.0 copy-done.9
  45.7 0.0 copy-start.10
  45.7 0.7 copy-done.10
  46.4 0.0 collective-permute-done.10.refs_7_
  46.4 0.0 copy-done.5
  46.4 0.0 copy-done.6
  46.4 0.0 copy-done.7
  46.4 0.0 copy-done.8
  46.4 14.5 %factor.1 = (f32[256,256]{1,0:T(8,128)}, bf16[1792,768]{1,0:T(8,128)(2,1)}) custom-call(f32[2,128,256]{2,1,0:T(8,128)} %pair.1.refs_0_, f32[2,128,256]{2,1,0:T(8,128)} %copy-done.8, f32[2,128,256]{2,1,0:T(8,128)} %copy-done.7, f32[2,128,256]{2,1,0:T(8,128)} %copy-done.9, f32[2,128,256]{2,1,0:T(8,128)} %copy-done.6, f32[2,128,256]{2,1,0:T(8,128)} %copy-done.10, ...), custom_call_target="tpu_custom_call" | custom-call | tf_op jit(solution)/shard_map/factor/pallas_call | solution.py:250
  60.9 0.0 copy-done.3
  60.9 11.5 %base.1 = (f32[4,128,256]{2,1,0:T(8,128)}, f32[4,128,1792]{2,1,0:T(8,128)}) custom-call(s32[16]{0:T(128)} %get-tuple-element.23.idx, f32[4,128,2048]{2,1,0:T(8,128)} %refs_1_.1, f32[4,128,2048]{2,1,0:T(8,128)} %refs_1_.1, f32[6,128,2048]{2,1,0:T(8,128)} %refs_9_.1, f32[6,128,2048]{2,1,0:T(8,128)} %refs_9_.1, f32[6,128,2048]{2,1,0:T(8,128)} %refs_9_.1, ...), custom_call_target="tpu_custom_call" | custom-call | tf_op jit(solution)/shard_map/base/pallas_call | solution.py:338
  72.4 0.0 collective-permute-done.11.came
  72.4 0.0 copy-start.2
  72.4 0.9 %copy-done.2 = f32[128,1792]{1,0:T(8,128)} copy-done((f32[128,1792]{1,0:T(8,128)}, f32[128,1792]{1,0:T(8,128)S(1)}, u32[]{:S(2)}) %copy-start.2) | copy-done | bytes 917528
  73.4 3.1 %add1.1.old = f32[4,128,1792]{2,1,0:T(8,128)} custom-call(s32[16]{0:T(128)} %get-tuple-element.23.idx, f32[4,128,1792]{2,1,0:T(8,128)} %get-tuple-element.40.old, f32[128,1792]{1,0:T(8,128)} %copy-done.2), custom_call_target="tpu_custom_call", output_to_operand_aliasing={{}: (1, {})} | custom-call | tf_op jit(solution)/shard_map/add1/pallas_call | solution.py:367
  76.5 0.0 collective-permute-done.12.came
  76.5 0.0 copy-start.1
  76.5 0.9 %copy-done.1 = f32[128,1792]{1,0:T(8,128)} copy-done((f32[128,1792]{1,0:T(8,128)}, f32[128,1792]{1,0:T(8,128)S(1)}, u32[]{:S(2)}) %copy-start.1) | copy-done | bytes 917528
  77.4 3.1 %add2.1.old = f32[4,128,1792]{2,1,0:T(8,128)} custom-call(s32[16]{0:T(128)} %get-tuple-element.23.idx, f32[4,128,1792]{2,1,0:T(8,128)} %add1.1.old, f32[128,1792]{1,0:T(8,128)} %copy-done.1), custom_call_target="tpu_custom_call", output_to_operand_aliasing={{}: (1, {})} | custom-call | tf_op jit(solution)/shard_map/add2/pallas_call | solution.py:367
  80.6 1.6 %collective-permute-done.13.came = f32[128,896]{1,0:T(8,128)S(1)} collective-permute-done((f32[128,896]{1,0:T(8,128)}, f32[128,896]{1,0:T(8,128)S(1)}, u32[]{:S(2)}, u32[]{:S(2)}) %collective-permute-start.13) | collective-permute-done | bytes 458784 | tf_op jit(solution)/shard_map/ppermute | solution.py:398
  82.2 0.0 copy-start.4
  82.2 0.8 copy-done.4
  83.0 2.6 %add3.1 = f32[4,128,1792]{2,1,0:T(8,128)} custom-call(s32[16]{0:T(128)} %get-tuple-element.23.idx, f32[4,128,1792]{2,1,0:T(8,128)} %add2.1.old, f32[128,896]{1,0:T(8,128)} %copy-done.4), custom_call_target="tpu_custom_call", output_to_operand_aliasing={{}: (1, {})} | custom-call | tf_op jit(solution)/shard_map/add3/pallas_call | solution.py:367
Async XLA Ops:
  3.3 7.6 %collective-permute-start.1 = (f32[128,256]{1,0:T(8,128)}, f32[128,256]{1,0:T(8,128)S(1)}, u32[]{:S(2)}, u32[]{:S(2)}) collective-permute-start(f32[128,256]{1,0:T(8,128)} %get-tuple-element.25.refs_0_), channel_id=1, source_target_pairs={{0,16},{1,17},{2,18},{3,19},{4,20},{5,21},{6,22},{7,23},{8,24},{9,... | collective-permute-start | bytes 393224 | tf_op jit(solution)/shard_map/ppermute | solution.py:398
  6.5 11.6 %collective-permute-start = (f32[2,128,256]{2,1,0:T(8,128)}, f32[2,128,256]{2,1,0:T(8,128)S(1)}, u32[]{:S(2)}, u32[]{:S(2)}) collective-permute-start(f32[2,128,256]{2,1,0:T(8,128)} %get-tuple-element.24), channel_id=1, source_target_pairs={{0,16},{1,17},{2,18},{3,19},{4,20},{5,21},{6,22},{7,23},{8,24},{9,... | collective-permute-start | bytes 786440 | tf_op jit(solution)/shard_map/ppermute | solution.py:398
  10.9 0.7 copy-start.11
  13.2 6.6 %collective-permute-start.2 = (f32[128,256]{1,0:T(8,128)}, f32[128,256]{1,0:T(8,128)S(1)}, u32[]{:S(2)}, u32[]{:S(2)}) collective-permute-start(f32[128,256]{1,0:T(8,128)} %get-tuple-element.30.refs_0_), channel_id=1, source_target_pairs={{0,8},{1,9},{2,10},{3,11},{4,12},{5,13},{6,14},{7,15},{8,0},{9,1},... | collective-permute-start | bytes 393224 | tf_op jit(solution)/shard_map/ppermute | solution.py:398
  15.2 25.0 %collective-permute-start.6 = (f32[128,1152]{1,0:T(8,128)}, f32[128,1152]{1,0:T(8,128)S(1)}, u32[]{:S(2)}, u32[]{:S(2)}) collective-permute-start(f32[128,1152]{1,0:T(8,128)} %get-tuple-element.31), channel_id=1, source_target_pairs={{0,16},{1,17},{2,18},{3,19},{4,20},{5,21},{6,22},{7,23},{8,24},{9,... | collective-permute-start | bytes 1769480 | tf_op jit(solution)/shard_map/ppermute | solution.py:398
  18.1 1.8 %copy-start = (f32[2,128,256]{2,1,0:T(8,128)}, f32[2,128,256]{2,1,0:T(8,128)S(1)}, u32[]{:S(2)}) copy-start(f32[2,128,256]{2,1,0:T(8,128)S(1)} %collective-permute-done.refs_2_.refs_10_) | copy-start | bytes 786436
  19.9 0.6 copy-start.12
  22.2 10.3 %collective-permute-start.5 = (f32[2,128,256]{2,1,0:T(8,128)}, f32[2,128,256]{2,1,0:T(8,128)S(1)}, u32[]{:S(2)}, u32[]{:S(2)}) collective-permute-start(f32[2,128,256]{2,1,0:T(8,128)} %pair.1.refs_0_), channel_id=1, source_target_pairs={{0,2},{1,3},{2,4},{3,5},{4,6},{5,7},{6,0},{7,1},{8,10},{9,11},{10,... | collective-permute-start | bytes 786440 | tf_op jit(solution)/shard_map/ppermute | solution.py:398
  24.2 48.2 %collective-permute-start.11 = (f32[128,1792]{1,0:T(8,128)}, f32[128,1792]{1,0:T(8,128)S(1)}, u32[]{:S(2)}, u32[]{:S(2)}) collective-permute-start(f32[128,1792]{1,0:T(8,128)} %get-tuple-element.41), channel_id=1, source_target_pairs={{0,16},{1,17},{2,18},{3,19},{4,20},{5,21},{6,22},{7,23},{8,24},{9,... | collective-permute-start | bytes 2752520 | tf_op jit(solution)/shard_map/ppermute | solution.py:398
  27.8 48.7 %collective-permute-start.12 = (f32[128,1792]{1,0:T(8,128)}, f32[128,1792]{1,0:T(8,128)S(1)}, u32[]{:S(2)}, u32[]{:S(2)}) collective-permute-start(f32[128,1792]{1,0:T(8,128)} %get-tuple-element.42), channel_id=1, source_target_pairs={{0,16},{1,17},{2,18},{3,19},{4,20},{5,21},{6,22},{7,23},{8,24},{9,... | collective-permute-start | bytes 2752520 | tf_op jit(solution)/shard_map/ppermute | solution.py:398
  27.8 10.2 %collective-permute-start.4 = (f32[2,128,256]{2,1,0:T(8,128)}, f32[2,128,256]{2,1,0:T(8,128)S(1)}, u32[]{:S(2)}, u32[]{:S(2)}) collective-permute-start(f32[2,128,256]{2,1,0:T(8,128)} %pair.1.refs_0_), channel_id=1, source_target_pairs={{0,4},{1,5},{2,6},{3,7},{4,0},{5,1},{6,2},{7,3},{8,12},{9,13},{10,... | collective-permute-start | bytes 786440 | tf_op jit(solution)/shard_map/ppermute | solution.py:398
  32.5 13.9 %copy-start.5 = (f32[2,128,256]{2,1,0:T(8,128)}, f32[2,128,256]{2,1,0:T(8,128)S(1)}, u32[]{:S(2)}) copy-start(f32[2,128,256]{2,1,0:T(8,128)S(1)} %collective-permute-done.5.refs_6_) | copy-start | bytes 786436
  32.5 7.7 %collective-permute-start.3 = (f32[2,128,256]{2,1,0:T(8,128)}, f32[2,128,256]{2,1,0:T(8,128)S(1)}, u32[]{:S(2)}, u32[]{:S(2)}) collective-permute-start(f32[2,128,256]{2,1,0:T(8,128)} %pair.1.refs_0_), channel_id=1, source_target_pairs={{0,6},{1,7},{2,0},{3,1},{4,2},{5,3},{6,4},{7,5},{8,14},{9,15},{10,... | collective-permute-start | bytes 786440 | tf_op jit(solution)/shard_map/ppermute | solution.py:398
  38.0 8.4 %copy-start.6 = (f32[2,128,256]{2,1,0:T(8,128)}, f32[2,128,256]{2,1,0:T(8,128)S(1)}, u32[]{:S(2)}) copy-start(f32[2,128,256]{2,1,0:T(8,128)S(1)} %collective-permute-done.4.refs_4_) | copy-start | bytes 786436
  40.2 6.2 %copy-start.7 = (f32[2,128,256]{2,1,0:T(8,128)}, f32[2,128,256]{2,1,0:T(8,128)S(1)}, u32[]{:S(2)}) copy-start(f32[2,128,256]{2,1,0:T(8,128)S(1)} %collective-permute-done.3.refs_2_) | copy-start | bytes 786436
  40.2 20.7 %copy-start.3 = (f32[128,1152]{1,0:T(8,128)}, f32[128,1152]{1,0:T(8,128)S(1)}, u32[]{:S(2)}) copy-start(f32[128,1152]{1,0:T(8,128)S(1)} %collective-permute-done.6.refs_11_) | copy-start | bytes 1769476
  40.2 3.9 %collective-permute-start.7 = (f32[2,128,256]{2,1,0:T(8,128)}, f32[2,128,256]{2,1,0:T(8,128)S(1)}, u32[]{:S(2)}, u32[]{:S(2)}) collective-permute-start(f32[2,128,256]{2,1,0:T(8,128)} %pair.1.refs_0_), channel_id=1, source_target_pairs={{0,1},{1,0},{2,3},{3,2},{4,5},{5,4},{6,7},{7,6},{8,9},{9,8},{10,11... | collective-permute-start | bytes 786440 | tf_op jit(solution)/shard_map/ppermute | solution.py:398
  40.3 3.9 %collective-permute-start.8 = (f32[2,128,256]{2,1,0:T(8,128)S(1)}, f32[2,128,256]{2,1,0:T(8,128)S(1)}, u32[]{:S(2)}, u32[]{:S(2)}) collective-permute-start(f32[2,128,256]{2,1,0:T(8,128)S(1)} %collective-permute-done.3.refs_2_), channel_id=1, source_target_pairs={{0,1},{1,0},{2,3},{3,2},{4,5},{5,4},{6,7},{7,6},{8,9},{9,8},{10,11... | collective-permute-start | bytes 786440 | tf_op jit(solution)/shard_map/ppermute | solution.py:398
  40.8 41.4 %collective-permute-start.13 = (f32[128,896]{1,0:T(8,128)}, f32[128,896]{1,0:T(8,128)S(1)}, u32[]{:S(2)}, u32[]{:S(2)}) collective-permute-start(f32[128,896]{1,0:T(8,128)} %get-tuple-element.43), channel_id=1, source_target_pairs={{0,16},{1,17},{2,18},{3,19},{4,20},{5,21},{6,22},{7,23},{8,24},{9,... | collective-permute-start | bytes 1376264 | tf_op jit(solution)/shard_map/ppermute | solution.py:398
  44.2 2.3 %copy-start.8 = (f32[2,128,256]{2,1,0:T(8,128)}, f32[2,128,256]{2,1,0:T(8,128)S(1)}, u32[]{:S(2)}) copy-start(f32[2,128,256]{2,1,0:T(8,128)S(1)} %collective-permute-done.7.refs_1_) | copy-start | bytes 786436
  44.2 1.5 %collective-permute-start.9 = (f32[2,128,256]{2,1,0:T(8,128)S(1)}, f32[2,128,256]{2,1,0:T(8,128)S(1)}, u32[]{:S(2)}, u32[]{:S(2)}) collective-permute-start(f32[2,128,256]{2,1,0:T(8,128)S(1)} %collective-permute-done.4.refs_4_), channel_id=1, source_target_pairs={{0,1},{1,0},{2,3},{3,2},{4,5},{5,4},{6,7},{7,6},{8,9},{9,8},{10,11... | collective-permute-start | bytes 786440 | tf_op jit(solution)/shard_map/ppermute | solution.py:398
  44.2 1.5 %copy-start.9 = (f32[2,128,256]{2,1,0:T(8,128)}, f32[2,128,256]{2,1,0:T(8,128)S(1)}, u32[]{:S(2)}) copy-start(f32[2,128,256]{2,1,0:T(8,128)S(1)} %collective-permute-done.8.refs_3_) | copy-start | bytes 786436
  44.2 2.2 %collective-permute-start.10 = (f32[2,128,256]{2,1,0:T(8,128)S(1)}, f32[2,128,256]{2,1,0:T(8,128)}, u32[]{:S(2)}, u32[]{:S(2)}) collective-permute-start(f32[2,128,256]{2,1,0:T(8,128)S(1)} %collective-permute-done.5.refs_6_), channel_id=1, source_target_pairs={{0,1},{1,0},{2,3},{3,2},{4,5},{5,4},{6,7},{7,6},{8,9},{9,8},{10,11... | collective-permute-start | bytes 786440 | tf_op jit(solution)/shard_map/ppermute | solution.py:398
  45.7 0.7 copy-start.10
  72.4 0.9 %copy-start.2 = (f32[128,1792]{1,0:T(8,128)}, f32[128,1792]{1,0:T(8,128)S(1)}, u32[]{:S(2)}) copy-start(f32[128,1792]{1,0:T(8,128)S(1)} %collective-permute-done.11.came) | copy-start | bytes 2752516
  76.5 0.9 %copy-start.1 = (f32[128,1792]{1,0:T(8,128)}, f32[128,1792]{1,0:T(8,128)S(1)}, u32[]{:S(2)}) copy-start(f32[128,1792]{1,0:T(8,128)S(1)} %collective-permute-done.12.came) | copy-start | bytes 2752516
  82.2 0.8 copy-start.4

commit v3 on v2

v3 whole, which is shorter than its diff:
```python
import functools

import jax
import jax.numpy as jnp
from jax import lax
from jax.experimental import pallas as pl
from jax.experimental.pallas import tpu as pltpu
from jax.sharding import PartitionSpec as P

PANEL = 256
BLK = 128
LANES = 128
HIGHEST = lax.Precision.HIGHEST
VMEM_LIMIT = 60 << 20
GROUP = 64
HEAD = 896
CHUNKS = ((0, 256, HEAD), (1, 256, 1792), (2, 256, 1792), (0, 256 + HEAD, 1792 - HEAD))

OUT = 0
SLOT = 4
KEEP = 8
CAME = 12
SMALL = pl.CostEstimate(flops=0, bytes_accessed=0, transcendentals=0)


def matmul(a, b, ca, cb):
    return lax.dot_general(
        a, b, (((ca,), (cb,)), ((), ())), precision=HIGHEST, preferred_element_type=jnp.float32
    )


def split(a):
    parts = []
    for _ in range(3):
        parts.append(a.astype(jnp.bfloat16))
        a = a - parts[-1].astype(jnp.float32)
    return parts


def any_space():
    return pl.BlockSpec(memory_space=pl.ANY)


def smem_space():
    return pl.BlockSpec(memory_space=pltpu.SMEM)


def params():
    return pltpu.CompilerParams(vmem_limit_bytes=VMEM_LIMIT)


def index_kernel(half, slots, maps, front, children, idx, piece, others, mine, theirs, old, kept, sem):
    dev = lax.axis_index("sub")
    sib = dev // half
    res = dev % half
    lead = pl.ds(0, PANEL)
    first = pltpu.make_async_copy(front.at[0, :, lead], old, sem.at[0])
    first.start()
    for step in range(8):
        mine[step] = -1
        theirs[step] = -1
    for b in range(slots):
        mine[(maps[sib, b * half + res] - res) // half] = b
        theirs[(maps[1 - sib, b * half + res] - res) // half] = b
    for i in range(16):
        idx[i] = -1
    n_out = jnp.int32(0)
    n_in = jnp.int32(0)
    none = jnp.int32(0)
    for q in range(4):
        b = mine[2 * q + 1 - sib]
        idx[OUT + n_out] = jnp.maximum(b, 0)
        n_out = n_out + jnp.where(b >= 0, 1, 0)
        idx[KEEP + q] = mine[2 * q + sib]
        t = theirs[2 * q + sib]
        idx[SLOT + n_in] = q
        idx[CAME + q] = jnp.where(t >= 0, n_in, -1)
        n_in = n_in + jnp.where(t >= 0, 1, 0)
        none = jnp.where(t >= 0, none, q)
    idx[SLOT + 3] = none
    keep = idx[KEEP]
    copies = [
        pltpu.make_async_copy(children.at[jnp.maximum(keep, 0), :, lead], kept, sem.at[1])
    ] + [
        pltpu.make_async_copy(children.at[idx[OUT + i], :, lead], out, sem.at[2 + i])
        for i, out in enumerate((others.at[0], others.at[1], others.at[2]))
    ]
    for copy in copies:
        copy.start()
    first.wait()
    for copy in copies:
        copy.wait()
    mine_at_0 = old[...] + kept[...] * jnp.where(keep >= 0, 1.0, 0.0)
    piece[...] = jnp.where(sib == 0, mine_at_0, others[0])


def make_indices(row_maps, front, children, half):
    vmem = pl.BlockSpec(memory_space=pltpu.VMEM)
    return pl.pallas_call(
        functools.partial(index_kernel, half, children.shape[0]),
        name="indices",
        out_shape=(
            jax.ShapeDtypeStruct((16,), jnp.int32),
            jax.ShapeDtypeStruct((BLK, PANEL), jnp.float32),
            jax.ShapeDtypeStruct((3, BLK, PANEL), jnp.float32),
        ),
        in_specs=[smem_space(), any_space(), any_space()],
        out_specs=(smem_space(), vmem, vmem),
        scratch_shapes=[
            pltpu.SMEM((8,), jnp.int32),
            pltpu.SMEM((8,), jnp.int32),
            pltpu.VMEM((BLK, PANEL), jnp.float32),
            pltpu.VMEM((BLK, PANEL), jnp.float32),
            pltpu.SemaphoreType.DMA((5,)),
        ],
        compiler_params=params(),
        cost_estimate=SMALL,
    )(row_maps, front, children)


def take_kernel(idx, children, *refs):
    outs, sem = refs[:-1], refs[-1]
    copies = []
    for i, (out, (which, low, width)) in enumerate(zip(outs, CHUNKS)):
        part = pl.ds(low, width)
        copies.append(pltpu.make_async_copy(children.at[idx[OUT + which], :, part], out, sem.at[i]))
    for copy in copies:
        copy.start()
    for copy in copies:
        copy.wait()


def take_blocks(idx, children):
    vmem = pl.BlockSpec(memory_space=pltpu.VMEM)
    return pl.pallas_call(
        take_kernel,
        name="take",
        out_shape=[jax.ShapeDtypeStruct((BLK, width), jnp.float32) for _, _, width in CHUNKS],
        in_specs=[smem_space(), any_space()],
        out_specs=[vmem for _ in CHUNKS],
        scratch_shapes=[pltpu.SemaphoreType.DMA((len(CHUNKS),))],
        compiler_params=params(),
        cost_estimate=SMALL,
    )(idx, children)


def inverse_factor(d):
    n = d.shape[0]
    row = lax.broadcasted_iota(jnp.int32, (n, n), 0)
    col = lax.broadcasted_iota(jnp.int32, (n, n), 1)
    m = jnp.concatenate([d, (row == col).astype(jnp.float32)], axis=1)
    w = 2 * n
    parts = n // 8
    groups = [m[8 * i : 8 * i + 8, :] for i in range(parts)]
    sub = lax.broadcasted_iota(jnp.int32, (8, w), 0)
    for q in range(parts):
        e = [
            [
                jnp.broadcast_to(groups[i][:, 8 * q + k : 8 * q + k + 1], (8, w))
                for i in range(q, parts)
            ]
            for k in range(8)
        ]
        for k in range(8):
            r = lax.rsqrt(jnp.broadcast_to(e[k][0][k : k + 1, :], (8, w)))
            pivot_row = jnp.broadcast_to(groups[q][k : k + 1, :], (8, w)) * r
            scaled = [v * r for v in e[k]]
            for i in range(q, parts):
                t = groups[i] - scaled[i - q] * pivot_row
                if i == q:
                    t = jnp.where(sub == k, pivot_row, jnp.where(sub > k, t, groups[i]))
                groups[i] = t
            for c in range(k + 1, 8):
                head = jnp.broadcast_to(e[c][0][k : k + 1, :], (8, w)) * r
                e[c] = [v - u * head for v, u in zip(e[c], scaled)]
    return jnp.concatenate(groups, axis=0)[:, n:]


def main_kernel(half, idx, *refs):
    pieces, (front, children, others, head), refs = refs[:8], refs[8:12], refs[12:]
    panel, update, window, m, base, kept, got, first, held, stage, sem = refs
    slots = base.shape[0]
    tiles = update.shape[2] // PANEL
    loads = [pltpu.make_async_copy(front, base, sem.at[0])]
    loads += [
        pltpu.make_async_copy(children.at[jnp.maximum(idx[KEEP + q], 0)], kept.at[q], sem.at[1 + q])
        for q in range(slots)
    ]
    loads += [
        pltpu.make_async_copy(others, got, sem.at[slots + 1]),
        pltpu.make_async_copy(head, first, sem.at[slots + 2]),
    ]
    for load in loads:
        load.start()

    dev = lax.axis_index("sub")
    h0 = (dev // 8) % 2
    z = (dev // 2) % 4
    core = dev % 2
    for i, ref in enumerate(pieces):
        zz = (z + i // 2) % 4
        cc = (core + i) % 2
        for h in range(2):
            block = ((h0 + h) % 2 * 4 + zz) * 2 + cc
            window[pl.ds(pl.multiple_of(block * BLK, BLK), BLK), :] = ref[h]
    s = window[0:PANEL, :]
    s = 0.5 * (s + s.T)
    m[:, :PANEL] = s
    row = lax.broadcasted_iota(jnp.int32, (PANEL, PANEL), 0)
    col = lax.broadcasted_iota(jnp.int32, (PANEL, PANEL), 1)
    m[:, PANEL:] = (row == col).astype(jnp.float32)
    for k in range(PANEL // GROUP):
        a, b = k * GROUP, (k + 1) * GROUP
        r = m[a:b, :]
        x = matmul(inverse_factor(r[:, a:b]), r, 1, 0)
        m[a:b, :] = x
        if b < PANEL:
            m[b:, :] = m[b:, :] - matmul(x[:, b:PANEL], x, 0, 0)

    for load in loads:
        load.wait()
    has = [jnp.where(idx[KEEP + q] >= 0, 1.0, 0.0) for q in range(slots)]
    leads = []
    for q in range(slots):
        which = idx[CAME + q]
        block = got[jnp.maximum(which, 0)] * jnp.where(which >= 0, 1.0, 0.0)
        leads.append(base[q, :, :PANEL] + kept[q, :, :PANEL] * has[q] + block)
    p = matmul(jnp.concatenate(leads, axis=0), m[:, PANEL:], 1, 1)
    stage[...] = p.reshape(stage.shape)
    saves = [pltpu.make_async_copy(stage, panel, sem.at[0])]
    saves[0].start()
    a, b, c = split(p)
    for i, part in enumerate((a, a, b, b, a, c)):
        held[:, i * PANEL : (i + 1) * PANEL] = part

    for t in range(tiles):
        low = PANEL * (t + 1)
        cols = slice(low, low + PANEL)
        a, b, c = split(matmul(window[cols, :], m[:, PANEL:], 1, 1))
        u = lax.dot_general(
            held[...],
            jnp.concatenate([a, b, a, b, c, a], axis=1),
            (((1,), (1,)), ((), ())),
            preferred_element_type=jnp.float32,
        )
        for q in range(slots):
            base[q, :, cols] = (
                base[q, :, cols] + kept[q, :, cols] * has[q] - u[q * BLK : (q + 1) * BLK, :]
            )
        width = min(max(HEAD + PANEL - low, 0), PANEL)
        if width:
            part = slice(low, low + width)
            base[0, :, part] = base[0, :, part] + first[:, low - PANEL : low - PANEL + width]
        saves.append(
            pltpu.make_async_copy(
                base.at[:, :, pl.ds(low, PANEL)],
                update.at[:, :, pl.ds(low - PANEL, PANEL)],
                sem.at[1 + t],
            )
        )
        saves[-1].start()
    for save in saves:
        save.wait()


def main(idx, pieces, front, children, others, head, half):
    slots, rows, columns = front.shape
    rest = columns - PANEL
    f32 = jnp.float32
    hbm = pl.BlockSpec(memory_space=pltpu.HBM)
    return pl.pallas_call(
        functools.partial(main_kernel, half),
        name="main",
        out_shape=(
            jax.ShapeDtypeStruct((slots, rows, PANEL), f32),
            jax.ShapeDtypeStruct((slots, rows, rest), f32),
        ),
        in_specs=[smem_space()]
        + [pl.BlockSpec(memory_space=pltpu.VMEM)] * 8
        + [hbm] * 4,
        out_specs=(hbm, hbm),
        scratch_shapes=[
            pltpu.VMEM((columns, PANEL), f32),
            pltpu.VMEM((PANEL, 2 * PANEL), f32),
            pltpu.VMEM((slots, rows, columns), f32),
            pltpu.VMEM((slots, rows, columns), f32),
            pltpu.VMEM(others.shape, f32),
            pltpu.VMEM(head.shape, f32),
            pltpu.VMEM((slots * rows, 6 * PANEL), jnp.bfloat16),
            pltpu.VMEM((slots, rows, PANEL), f32),
            pltpu.SemaphoreType.DMA((8,)),
        ],
        compiler_params=params(),
        cost_estimate=SMALL,
    )(idx, *pieces, front, children, others, head)


def add_block(idx, update, came, which):
    block, low, width = CHUNKS[which]
    at = (idx[SLOT + block], 0, low - PANEL)
    old = lax.dynamic_slice(update, at, (1, BLK, width))
    return lax.dynamic_update_slice(update, old + came[None], at)


def route(move, keep=lambda x: True):
    pairs = []
    for x in range(4):
        if keep(x):
            for z in range(4):
                for c in range(2):
                    tx, tz, tc = move(x, z, c)
                    pairs.append(((x * 4 + z) * 2 + c, (tx * 4 + tz) * 2 + tc))
    return pairs


OPPOSITE = route(lambda x, z, c: ((x + 2) % 4, z, c))
X_UP = route(lambda x, z, c: ((x + 1) % 4, z, c))
X_DOWN = route(lambda x, z, c: ((x + 3) % 4, z, c))
Z_UP = route(lambda x, z, c: (x, (z + 1) % 4, c))
Z_DOWN = route(lambda x, z, c: (x, (z + 3) % 4, c))
Z_FAR = route(lambda x, z, c: (x, (z + 2) % 4, c))
CORE = route(lambda x, z, c: (x, z, 1 - c))


def send(value, pairs):
    return lax.ppermute(value, "sub", pairs)


def per_device(front, children, row_maps):
    half = lax.axis_size("sub") // 2
    columns = front.shape[2]

    idx, piece, panels = make_indices(row_maps, front, children, half)
    came_piece = send(piece, OPPOSITE)
    blocks = take_blocks(idx, children)
    came_panels = send(panels, OPPOSITE)

    came_piece, *blocks = lax.optimization_barrier((came_piece, *blocks))
    lead = piece + came_piece
    came = [send(b, OPPOSITE) for b in blocks]
    above = send(lead[: BLK // 2], X_UP)
    below = send(lead[BLK // 2 :], X_DOWN)
    own = jnp.stack([lead, jnp.concatenate([above, below])])
    own, came_panels = lax.optimization_barrier((own, came_panels))

    by_z = [own, send(own, Z_DOWN), send(own, Z_FAR), send(own, Z_UP)]
    *by_z, came[0] = lax.optimization_barrier((*by_z, came[0]))
    pieces = []
    for v in by_z:
        pieces += [v, send(v, CORE)]
    panel, update = main(idx, pieces, front, children, came_panels, came[0], half)
    for which in range(1, len(CHUNKS)):
        update = add_block(idx, update, came[which], which)
    return panel, update


def solution(mesh):
    placed = (P("front", "sub", None), P("front", "sub", None), P("front", None))
    return jax.shard_map(
        per_device,
        mesh=mesh,
        in_specs=placed,
        out_specs=(P("front", "sub", None), P("front", "sub", None)),
        check_vma=False,
    )
```

time: 86.1 us -> 81.6 us (0.948)
  Pallas kernels: 44.9 us -> 27.6 us
  waiting for transfers between devices: 10.1 us -> 17.2 us
  other arithmetic: 0 us -> 6.28 us
  between operations: 0.74 us -> 6.71 us
  starting transfers between devices: 25.2 us -> 21.9 us
  local copies, waits for them, and re-layouts: 4.64 us -> 1.4 us
    pallas_call x7 -> x1, Pallas kernels: 38.2 us -> 20.8 us  [main(): pl.pallas_call(functools.partial(main_kernel, half), name='main', out_sha...]
    ppermute x14 -> x15, waiting for transfers between devices: 10.1 us -> 17.2 us  [send(): return lax.ppermute(value, 'sub', pairs)]
    dynamic_update_slice x0 -> x3, other arithmetic: none -> 6.23 us  [add_block(): return lax.dynamic_update_slice(update, old + came[None], at)]
    unnamed x26 -> x16, local copies, waits for them, and re-layouts: 4.64 us -> 0.74 us
    ppermute x14 -> x15, starting transfers between devices: 25.2 us -> 21.9 us  [send(): return lax.ppermute(value, 'sub', pairs)]
  transfers between devices with their start and end apart: 14 -> 15, of which waited for: 6 -> 5; matrix products, arithmetic and copies ran while one was open for 0% -> 6% of each run, Pallas kernels for 46% -> 31%
where the time goes in v3:
time: 81.6 us; the launch traced here: 81.1 us
  Pallas kernels  27.6 us (34%)
  starting transfers between devices  21.9 us (27%)
  waiting for transfers between devices  17.2 us (21%)
  between operations  6.71 us (8%)
  other arithmetic  6.28 us (8%)
  local copies, waits for them, and re-layouts  1.4 us (2%)
    ppermute x15, starting transfers between devices, send(): return lax.ppermute(value, 'sub', pairs)  21.9 us
    pallas_call x1, Pallas kernels, main(): pl.pallas_call(functools.partial(main_kernel, half), name='main', out_sha...  20.8 us
    ppermute x15, waiting for transfers between devices, send(): return lax.ppermute(value, 'sub', pairs)  17.2 us
    dynamic_update_slice x3, other arithmetic, add_block(): return lax.dynamic_update_slice(update, old + came[None], at)  6.23 us
    pallas_call x1, Pallas kernels, take_blocks(): pl.pallas_call(take_kernel, name='take', out_shape=[jax.ShapeDtypeStruct(...  4.01 us
    pallas_call x1, Pallas kernels, make_indices(): pl.pallas_call(functools.partial(index_kernel, half, children.shape[0]),...  2.73 us
  transfers between devices with their start and end apart: 15, of which 5 were waited for; matrix products, arithmetic and copies ran while one was open for 6% of the time, Pallas kernels for 31%

profile of v3, /device:TPU:0, one launch (start us, length us, event | category | flops | bytes accessed | tf_op | source)
XLA Modules:
  0.0 81.1 jit_solution(9326508636546903959)
XLA Ops:
  0.6 2.7 %indices.1 = (s32[16]{0:T(128)}, f32[128,256]{1,0:T(8,128)}, f32[3,128,256]{2,1,0:T(8,128)}) custom-call(s32[2,96]{1,0:T(2,128)} %maps.1, f32[4,128,2048]{2,1,0:T(8,128)} %refs_8_.1, f32[6,128,2048]{2,1,0:T(8,128)} %refs_9_.1), custom_call_target="tpu_custom_call" | custom-call | tf_op jit(solution)/shard_map/indices/pallas_call | solution.py:99
  3.4 0.0 copy-start.6
  3.4 3.2 %collective-permute-start = (f32[128,256]{1,0:T(8,128)}, f32[128,256]{1,0:T(8,128)S(1)}, u32[]{:S(2)}, u32[]{:S(2)}) collective-permute-start(f32[128,256]{1,0:T(8,128)} %get-tuple-element.24), channel_id=1, source_target_pairs={{0,16},{1,17},{2,18},{3,19},{4,20},{5,21},{6,22},{7,23},{8,24},{9,... | collective-permute-start | bytes 393224 | tf_op jit(solution)/shard_map/ppermute | solution.py:326
  6.6 0.4 collective-permute-start.3
  7.0 0.0 copy-start.7
  7.0 4.0 %take.1 = (f32[128,896]{1,0:T(8,128)}, f32[128,1792]{1,0:T(8,128)}, f32[128,1792]{1,0:T(8,128)}, f32[128,896]{1,0:T(8,128)}) custom-call(s32[16]{0:T(128)} %get-tuple-element.23.idx, f32[6,128,2048]{2,1,0:T(8,128)} %refs_9_.1), custom_call_target="tpu_custom_call" | custom-call | tf_op jit(solution)/shard_map/take/pallas_call | solution.py:135
  11.0 0.0 collective-permute-done
  11.0 0.0 copy-done.6
  11.1 2.0 %collective-permute-start.1 = (f32[64,256]{1,0:T(8,128)S(1)}, f32[64,256]{1,0:T(8,128)S(1)}, u32[]{:S(2)}, u32[]{:S(2)}) collective-permute-start(f32[64,256]{1,0:T(8,128)S(1)} %get-tuple-element.44), channel_id=1, source_target_pairs={{0,8},{1,9},{2,10},{3,11},{4,12},{5,13},{6,14},{7,15},{8,16},{9,17... | collective-permute-start | bytes 196616 | tf_op jit(solution)/shard_map/ppermute | solution.py:326
  13.1 1.5 %collective-permute-start.2 = (f32[64,256]{1,0:T(8,128)S(1)}, f32[64,256]{1,0:T(8,128)S(1)}, u32[]{:S(2)}, u32[]{:S(2)}) collective-permute-start(f32[64,256]{1,0:T(8,128)S(1)} %get-tuple-element.45), channel_id=1, source_target_pairs={{0,24},{1,25},{2,26},{3,27},{4,28},{5,29},{6,30},{7,31},{8,0},{9,1... | collective-permute-start | bytes 196616 | tf_op jit(solution)/shard_map/ppermute | solution.py:326
  14.6 2.2 %collective-permute-start.7 = (f32[128,896]{1,0:T(8,128)}, f32[128,896]{1,0:T(8,128)S(1)}, u32[]{:S(2)}, u32[]{:S(2)}) collective-permute-start(f32[128,896]{1,0:T(8,128)} %get-tuple-element.32), channel_id=1, source_target_pairs={{0,16},{1,17},{2,18},{3,19},{4,20},{5,21},{6,22},{7,23},{8,24},{9,... | collective-permute-start | bytes 1376264 | tf_op jit(solution)/shard_map/ppermute | solution.py:326
  16.8 1.3 %collective-permute-start.12 = (f32[128,1792]{1,0:T(8,128)}, f32[128,1792]{1,0:T(8,128)S(1)}, u32[]{:S(2)}, u32[]{:S(2)}) collective-permute-start(f32[128,1792]{1,0:T(8,128)} %get-tuple-element.41), channel_id=1, source_target_pairs={{0,16},{1,17},{2,18},{3,19},{4,20},{5,21},{6,22},{7,23},{8,24},{9,... | collective-permute-start | bytes 2752520 | tf_op jit(solution)/shard_map/ppermute | solution.py:326
  18.1 3.6 %collective-permute-done.1 = f32[64,256]{1,0:T(8,128)S(1)} collective-permute-done((f32[64,256]{1,0:T(8,128)S(1)}, f32[64,256]{1,0:T(8,128)S(1)}, u32[]{:S(2)}, u32[]{:S(2)}) %collective-permute-start.1) | collective-permute-done | bytes 65568 | tf_op jit(solution)/shard_map/ppermute | solution.py:326
  21.7 0.0 collective-permute-done.2
  21.7 0.0 copy-start
  21.7 0.0 collective-permute-done.3.refs_10_
  21.7 0.0 copy-start.2
  21.8 2.0 %collective-permute-start.6 = (f32[2,128,256]{2,1,0:T(8,128)S(1)}, f32[2,128,256]{2,1,0:T(8,128)S(1)}, u32[]{:S(2)}, u32[]{:S(2)}) collective-permute-start(f32[2,128,256]{2,1,0:T(8,128)S(1)} %pad_maximum_fusion.refs_0_), channel_id=1, source_target_pairs={{0,2},{1,3},{2,4},{3,5},{4,6},{5,7},{6,0},{7,1},{8,10},{9,11},{10,... | collective-permute-start | bytes 786440 | tf_op jit(solution)/shard_map/ppermute | solution.py:326
  23.7 3.6 %collective-permute-start.5 = (f32[2,128,256]{2,1,0:T(8,128)S(1)}, f32[2,128,256]{2,1,0:T(8,128)S(1)}, u32[]{:S(2)}, u32[]{:S(2)}) collective-permute-start(f32[2,128,256]{2,1,0:T(8,128)S(1)} %pad_maximum_fusion.refs_0_), channel_id=1, source_target_pairs={{0,4},{1,5},{2,6},{3,7},{4,0},{5,1},{6,2},{7,3},{8,12},{9,13},{10,... | collective-permute-start | bytes 786440 | tf_op jit(solution)/shard_map/ppermute | solution.py:326
  27.3 1.0 %collective-permute-start.4 = (f32[2,128,256]{2,1,0:T(8,128)S(1)}, f32[2,128,256]{2,1,0:T(8,128)}, u32[]{:S(2)}, u32[]{:S(2)}) collective-permute-start(f32[2,128,256]{2,1,0:T(8,128)S(1)} %pad_maximum_fusion.refs_0_), channel_id=1, source_target_pairs={{0,6},{1,7},{2,0},{3,1},{4,2},{5,3},{6,4},{7,5},{8,14},{9,15},{10,... | collective-permute-start | bytes 786440 | tf_op jit(solution)/shard_map/ppermute | solution.py:326
  28.3 3.3 %collective-permute-done.7.refs_11_ = f32[128,896]{1,0:T(8,128)S(1)} collective-permute-done((f32[128,896]{1,0:T(8,128)}, f32[128,896]{1,0:T(8,128)S(1)}, u32[]{:S(2)}, u32[]{:S(2)}) %collective-permute-start.7) | collective-permute-done | bytes 458784 | tf_op jit(solution)/shard_map/ppermute | solution.py:326
  31.6 0.0 copy-start.1
  31.6 0.7 collective-permute-done.6.refs_6_
  32.3 0.0 copy-start.3
  32.3 6.8 %collective-permute-done.5.refs_4_ = f32[2,128,256]{2,1,0:T(8,128)S(1)} collective-permute-done((f32[2,128,256]{2,1,0:T(8,128)S(1)}, f32[2,128,256]{2,1,0:T(8,128)S(1)}, u32[]{:S(2)}, u32[]{:S(2)}) %collective-permute-start.5) | collective-permute-done | bytes 262176 | tf_op jit(solution)/shard_map/ppermute | solution.py:326
  39.0 0.0 copy-start.4
  39.0 0.0 collective-permute-done.4.refs_2_
  39.1 0.0 collective-permute-start.8
  39.1 2.8 %collective-permute-start.13 = (f32[128,1792]{1,0:T(8,128)}, f32[128,1792]{1,0:T(8,128)S(1)}, u32[]{:S(2)}, u32[]{:S(2)}) collective-permute-start(f32[128,1792]{1,0:T(8,128)} %get-tuple-element.42), channel_id=1, source_target_pairs={{0,16},{1,17},{2,18},{3,19},{4,20},{5,21},{6,22},{7,23},{8,24},{9,... | collective-permute-start | bytes 2752520 | tf_op jit(solution)/shard_map/ppermute | solution.py:326
  41.9 0.2 collective-permute-start.9
  42.1 0.3 collective-permute-start.10
  42.4 0.0 collective-permute-done.8.refs_1_
  42.4 0.0 copy-start.5
  42.4 0.7 copy-done.5
  43.1 0.2 collective-permute-start.11
  43.3 0.0 copy-done.7
  43.3 0.7 fusion.4
  49.9 0.0 collective-permute-done.9.refs_3_
  49.9 1.2 %collective-permute-start.14 = (f32[128,896]{1,0:T(8,128)}, f32[128,896]{1,0:T(8,128)S(1)}, u32[]{:S(2)}, u32[]{:S(2)}) collective-permute-start(f32[128,896]{1,0:T(8,128)} %get-tuple-element.43), channel_id=1, source_target_pairs={{0,16},{1,17},{2,18},{3,19},{4,20},{5,21},{6,22},{7,23},{8,24},{9,... | collective-permute-start | bytes 1376264 | tf_op jit(solution)/shard_map/ppermute | solution.py:326
  51.1 0.0 collective-permute-done.10.refs_5_
  51.1 0.0 collective-permute-done.11.refs_7_
  51.1 0.0 copy-done
  51.1 0.0 copy-done.2
  51.1 0.0 copy-done.1
  51.1 0.0 copy-done.3
  51.1 0.0 copy-done.4
  51.1 20.8 %main.1 = (f32[4,128,256]{2,1,0:T(8,128)}, f32[4,128,1792]{2,1,0:T(8,128)}) custom-call(s32[16]{0:T(128)} %get-tuple-element.23.idx, f32[2,128,256]{2,1,0:T(8,128)} %copy-done, f32[2,128,256]{2,1,0:T(8,128)} %copy-done.5, f32[2,128,256]{2,1,0:T(8,128)} %collective-permute-done.4.refs_2_, f32[2,128,256]{2,1,0:T(8,128)} %collective-permute-done.9.refs_3_, ...), custom_call_target="tpu_custom_call" | custom-call | tf_op jit(solution)/shard_map/main/pallas_call | solution.py:271
  72.0 0.0 collective-permute-done.12
  72.0 2.2 %fusion.1 = f32[4,128,1792]{2,1,0:T(8,128)} fusion(f32[4,128,1792]{2,1,0:T(8,128)} %get-tuple-element.40, s32[]{:T(128)S(6)} %select_n.12, f32[128,1792]{1,0:T(8,128)S(1)} %collective-permute-done.12), kind=kLoop, calls=%fused_computation.3 | loop fusion | flops 229376 | bytes 2752516 | tf_op jit(solution)/shard_map/dynamic_update_slice | solution.py:302
  74.2 0.0 collective-permute-done.13
  74.2 2.2 %fusion = f32[4,128,1792]{2,1,0:T(8,128)} fusion(f32[4,128,1792]{2,1,0:T(8,128)} %fusion.1, s32[]{:T(128)S(6)} %select_n.13, f32[128,1792]{1,0:T(8,128)S(1)} %collective-permute-done.13), kind=kLoop, calls=%fused_computation.1 | loop fusion | flops 229376 | bytes 2752516 | tf_op jit(solution)/shard_map/dynamic_update_slice | solution.py:302
  76.4 2.9 %collective-permute-done.14 = f32[128,896]{1,0:T(8,128)S(1)} collective-permute-done((f32[128,896]{1,0:T(8,128)}, f32[128,896]{1,0:T(8,128)S(1)}, u32[]{:S(2)}, u32[]{:S(2)}) %collective-permute-start.14) | collective-permute-done | bytes 458784 | tf_op jit(solution)/shard_map/ppermute | solution.py:326
  79.3 1.8 %fusion.2 = f32[4,128,1792]{2,1,0:T(8,128)} fusion(f32[4,128,1792]{2,1,0:T(8,128)} %fusion, s32[]{:T(128)S(6)} %select_n.14, f32[128,896]{1,0:T(8,128)S(1)} %collective-permute-done.14), kind=kLoop, calls=%fused_computation.5 | loop fusion | flops 114688 | bytes 1376260 | tf_op jit(solution)/shard_map/dynamic_update_slice | solution.py:302
  (4 shorter events, 0.1 us)
Async XLA Ops:
  3.4 7.6 %copy-start.6 = (f32[128,256]{1,0:T(8,128)S(1)}, f32[128,256]{1,0:T(8,128)}, u32[]{:S(2)}) copy-start(f32[128,256]{1,0:T(8,128)} %get-tuple-element.24) | copy-start | bytes 393220
  3.4 7.6 %collective-permute-start = (f32[128,256]{1,0:T(8,128)}, f32[128,256]{1,0:T(8,128)S(1)}, u32[]{:S(2)}, u32[]{:S(2)}) collective-permute-start(f32[128,256]{1,0:T(8,128)} %get-tuple-element.24), channel_id=1, source_target_pairs={{0,16},{1,17},{2,18},{3,19},{4,20},{5,21},{6,22},{7,23},{8,24},{9,... | collective-permute-start | bytes 393224 | tf_op jit(solution)/shard_map/ppermute | solution.py:326
  6.6 15.2 %collective-permute-start.3 = (f32[3,128,256]{2,1,0:T(8,128)}, f32[3,128,256]{2,1,0:T(8,128)S(1)}, u32[]{:S(2)}, u32[]{:S(2)}) collective-permute-start(f32[3,128,256]{2,1,0:T(8,128)} %get-tuple-element.30), channel_id=1, source_target_pairs={{0,16},{1,17},{2,18},{3,19},{4,20},{5,21},{6,22},{7,23},{8,24},{9,... | collective-permute-start | bytes 1179656 | tf_op jit(solution)/shard_map/ppermute | solution.py:326
  7.0 36.3 %copy-start.7 = (s32[16]{0:T(128)S(1)}, s32[16]{0:T(128)}, u32[]{:S(2)}) copy-start(s32[16]{0:T(128)} %get-tuple-element.23.idx) | copy-start | bytes 196
  11.1 10.6 %collective-permute-start.1 = (f32[64,256]{1,0:T(8,128)S(1)}, f32[64,256]{1,0:T(8,128)S(1)}, u32[]{:S(2)}, u32[]{:S(2)}) collective-permute-start(f32[64,256]{1,0:T(8,128)S(1)} %get-tuple-element.44), channel_id=1, source_target_pairs={{0,8},{1,9},{2,10},{3,11},{4,12},{5,13},{6,14},{7,15},{8,16},{9,17... | collective-permute-start | bytes 196616 | tf_op jit(solution)/shard_map/ppermute | solution.py:326
  13.1 8.6 %collective-permute-start.2 = (f32[64,256]{1,0:T(8,128)S(1)}, f32[64,256]{1,0:T(8,128)S(1)}, u32[]{:S(2)}, u32[]{:S(2)}) collective-permute-start(f32[64,256]{1,0:T(8,128)S(1)} %get-tuple-element.45), channel_id=1, source_target_pairs={{0,24},{1,25},{2,26},{3,27},{4,28},{5,29},{6,30},{7,31},{8,0},{9,1... | collective-permute-start | bytes 196616 | tf_op jit(solution)/shard_map/ppermute | solution.py:326
  14.6 17.0 %collective-permute-start.7 = (f32[128,896]{1,0:T(8,128)}, f32[128,896]{1,0:T(8,128)S(1)}, u32[]{:S(2)}, u32[]{:S(2)}) collective-permute-start(f32[128,896]{1,0:T(8,128)} %get-tuple-element.32), channel_id=1, source_target_pairs={{0,16},{1,17},{2,18},{3,19},{4,20},{5,21},{6,22},{7,23},{8,24},{9,... | collective-permute-start | bytes 1376264 | tf_op jit(solution)/shard_map/ppermute | solution.py:326
  16.8 55.2 %collective-permute-start.12 = (f32[128,1792]{1,0:T(8,128)}, f32[128,1792]{1,0:T(8,128)S(1)}, u32[]{:S(2)}, u32[]{:S(2)}) collective-permute-start(f32[128,1792]{1,0:T(8,128)} %get-tuple-element.41), channel_id=1, source_target_pairs={{0,16},{1,17},{2,18},{3,19},{4,20},{5,21},{6,22},{7,23},{8,24},{9,... | collective-permute-start | bytes 2752520 | tf_op jit(solution)/shard_map/ppermute | solution.py:326
  21.7 29.3 %copy-start = (f32[2,128,256]{2,1,0:T(8,128)}, f32[2,128,256]{2,1,0:T(8,128)S(1)}, u32[]{:S(2)}) copy-start(f32[2,128,256]{2,1,0:T(8,128)S(1)} %pad_maximum_fusion.refs_0_) | copy-start | bytes 786436
  21.7 29.3 %copy-start.2 = (f32[3,128,256]{2,1,0:T(8,128)}, f32[3,128,256]{2,1,0:T(8,128)S(1)}, u32[]{:S(2)}) copy-start(f32[3,128,256]{2,1,0:T(8,128)S(1)} %collective-permute-done.3.refs_10_) | copy-start | bytes 1179652
  21.8 10.5 %collective-permute-start.6 = (f32[2,128,256]{2,1,0:T(8,128)S(1)}, f32[2,128,256]{2,1,0:T(8,128)S(1)}, u32[]{:S(2)}, u32[]{:S(2)}) collective-permute-start(f32[2,128,256]{2,1,0:T(8,128)S(1)} %pad_maximum_fusion.refs_0_), channel_id=1, source_target_pairs={{0,2},{1,3},{2,4},{3,5},{4,6},{5,7},{6,0},{7,1},{8,10},{9,11},{10,... | collective-permute-start | bytes 786440 | tf_op jit(solution)/shard_map/ppermute | solution.py:326
  23.7 15.3 %collective-permute-start.5 = (f32[2,128,256]{2,1,0:T(8,128)S(1)}, f32[2,128,256]{2,1,0:T(8,128)S(1)}, u32[]{:S(2)}, u32[]{:S(2)}) collective-permute-start(f32[2,128,256]{2,1,0:T(8,128)S(1)} %pad_maximum_fusion.refs_0_), channel_id=1, source_target_pairs={{0,4},{1,5},{2,6},{3,7},{4,0},{5,1},{6,2},{7,3},{8,12},{9,13},{10,... | collective-permute-start | bytes 786440 | tf_op jit(solution)/shard_map/ppermute | solution.py:326
  27.3 11.7 %collective-permute-start.4 = (f32[2,128,256]{2,1,0:T(8,128)S(1)}, f32[2,128,256]{2,1,0:T(8,128)}, u32[]{:S(2)}, u32[]{:S(2)}) collective-permute-start(f32[2,128,256]{2,1,0:T(8,128)S(1)} %pad_maximum_fusion.refs_0_), channel_id=1, source_target_pairs={{0,6},{1,7},{2,0},{3,1},{4,2},{5,3},{6,4},{7,5},{8,14},{9,15},{10,... | collective-permute-start | bytes 786440 | tf_op jit(solution)/shard_map/ppermute | solution.py:326
  31.6 19.5 %copy-start.1 = (f32[128,896]{1,0:T(8,128)}, f32[128,896]{1,0:T(8,128)S(1)}, u32[]{:S(2)}) copy-start(f32[128,896]{1,0:T(8,128)S(1)} %collective-permute-done.7.refs_11_) | copy-start | bytes 1376260
  32.3 18.8 %copy-start.3 = (f32[2,128,256]{2,1,0:T(8,128)}, f32[2,128,256]{2,1,0:T(8,128)S(1)}, u32[]{:S(2)}) copy-start(f32[2,128,256]{2,1,0:T(8,128)S(1)} %collective-permute-done.6.refs_6_) | copy-start | bytes 786436
  39.0 12.1 %copy-start.4 = (f32[2,128,256]{2,1,0:T(8,128)}, f32[2,128,256]{2,1,0:T(8,128)S(1)}, u32[]{:S(2)}) copy-start(f32[2,128,256]{2,1,0:T(8,128)S(1)} %collective-permute-done.5.refs_4_) | copy-start | bytes 786436
  39.1 3.4 %collective-permute-start.8 = (f32[2,128,256]{2,1,0:T(8,128)S(1)}, f32[2,128,256]{2,1,0:T(8,128)S(1)}, u32[]{:S(2)}, u32[]{:S(2)}) collective-permute-start(f32[2,128,256]{2,1,0:T(8,128)S(1)} %pad_maximum_fusion.refs_0_), channel_id=1, source_target_pairs={{0,1},{1,0},{2,3},{3,2},{4,5},{5,4},{6,7},{7,6},{8,9},{9,8},{10,11... | collective-permute-start | bytes 786440 | tf_op jit(solution)/shard_map/ppermute | solution.py:326
  39.1 35.1 %collective-permute-start.13 = (f32[128,1792]{1,0:T(8,128)}, f32[128,1792]{1,0:T(8,128)S(1)}, u32[]{:S(2)}, u32[]{:S(2)}) collective-permute-start(f32[128,1792]{1,0:T(8,128)} %get-tuple-element.42), channel_id=1, source_target_pairs={{0,16},{1,17},{2,18},{3,19},{4,20},{5,21},{6,22},{7,23},{8,24},{9,... | collective-permute-start | bytes 2752520 | tf_op jit(solution)/shard_map/ppermute | solution.py:326
  41.9 8.0 %collective-permute-start.9 = (f32[2,128,256]{2,1,0:T(8,128)}, f32[2,128,256]{2,1,0:T(8,128)}, u32[]{:S(2)}, u32[]{:S(2)}) collective-permute-start(f32[2,128,256]{2,1,0:T(8,128)} %collective-permute-done.4.refs_2_), channel_id=1, source_target_pairs={{0,1},{1,0},{2,3},{3,2},{4,5},{5,4},{6,7},{7,6},{8,9},{9,8},{10,11... | collective-permute-start | bytes 786440 | tf_op jit(solution)/shard_map/ppermute | solution.py:326
  42.1 9.0 %collective-permute-start.10 = (f32[2,128,256]{2,1,0:T(8,128)S(1)}, f32[2,128,256]{2,1,0:T(8,128)}, u32[]{:S(2)}, u32[]{:S(2)}) collective-permute-start(f32[2,128,256]{2,1,0:T(8,128)S(1)} %collective-permute-done.5.refs_4_), channel_id=1, source_target_pairs={{0,1},{1,0},{2,3},{3,2},{4,5},{5,4},{6,7},{7,6},{8,9},{9,8},{10,11... | collective-permute-start | bytes 786440 | tf_op jit(solution)/shard_map/ppermute | solution.py:326
  42.4 0.7 copy-start.5
  43.1 7.9 %collective-permute-start.11 = (f32[2,128,256]{2,1,0:T(8,128)S(1)}, f32[2,128,256]{2,1,0:T(8,128)}, u32[]{:S(2)}, u32[]{:S(2)}) collective-permute-start(f32[2,128,256]{2,1,0:T(8,128)S(1)} %collective-permute-done.6.refs_6_), channel_id=1, source_target_pairs={{0,1},{1,0},{2,3},{3,2},{4,5},{5,4},{6,7},{7,6},{8,9},{9,8},{10,11... | collective-permute-start | bytes 786440 | tf_op jit(solution)/shard_map/ppermute | solution.py:326
  49.9 29.4 %collective-permute-start.14 = (f32[128,896]{1,0:T(8,128)}, f32[128,896]{1,0:T(8,128)S(1)}, u32[]{:S(2)}, u32[]{:S(2)}) collective-permute-start(f32[128,896]{1,0:T(8,128)} %get-tuple-element.43), channel_id=1, source_target_pairs={{0,16},{1,17},{2,18},{3,19},{4,20},{5,21},{6,22},{7,23},{8,24},{9,... | collective-permute-start | bytes 1376264 | tf_op jit(solution)/shard_map/ppermute | solution.py:326
